TPU v7x, 512 devices: a whole 4x8x8 slice. The times are simulated.
512 devices in a mesh: dp: 64 (over y, z), tm: 8 (over x, core).
Axes of the slice: x: 4, y: 8, z: 8, core: 2. Of those that a mesh axis runs over, the one named last changes fastest.
Arguments:
- latents: bfloat16 [16384, 48, 1024], P('dp', 'tm'), may hold values from -6 to 6
- lengths: int32 [16384], P('dp'), may hold values from 1 to 48, as said below
- plan: int32 [16384], P('dp'), may hold values from 0 to 255, as said below
- w_in: bfloat16 [1024, 1024], P(None, 'dp'), may hold values from -0.1875 to 0.1875
- w_down: bfloat16 [1024, 64], replicated, may hold values from -0.1875 to 0.1875
- w_up: bfloat16 [64, 1024], replicated, may hold values from -0.75 to 0.75
- w_out: bfloat16 [1024, 1024], P(None, 'dp'), may hold values from -0.1875 to 0.1875
- rate: float32 [1024], replicated, may hold values from 0.004 to 1.5
- gain: float32 [1024], replicated, may hold values from 0.5 to 1.5
- w_bits: bfloat16 [1024, 18], replicated, may hold values from -0.1875 to 0.1875
Outputs:
- codes: bfloat16 [18, 48, 16384], P(None, 'tm', 'dp')
- penalty: float32 [], replicated
Inputs may be any that keep to these rules, and one draw needn't show every extreme that they name: `plan`: each aligned block of 256 entries is a permutation of 0 to 255. The rows of each aligned block of 256 rows share a cap on their lengths that rises with the block's index from about a third of 48 to 48; the first row of each block has exactly its cap.
All inputs are finite; a program needn't handle non-finite values.
Results may differ from a plain program's by a relative error of at most 0.0056.
Values may be sent and summed in bfloat16 or wider, within the bound.
A program may use at most 128 MiB of HBM per device.

v0:
```python
import jax
import jax.numpy as jnp
from jax import lax
from jax.sharding import PartitionSpec as P


def passed_along(value, axis, steps):
    count = lax.axis_size(axis)
    initial, last = (max(0, -steps), min(count, count - steps))
    return lax.ppermute(value, axis, [(source, source + steps) for source in range(initial, last)])


def bit_entropy(logit_values):
    scaled = 4.0 * logit_values
    chance = jax.nn.sigmoid(scaled)
    return chance * jax.nn.softplus(-scaled) + (1.0 - chance) * jax.nn.softplus(scaled)


def shards(latents, lengths, plan, w_in, w_down, w_up, w_out, rate, gain, w_bits):
    row_count, frame_count, feature_width = latents.shape
    senders = lax.axis_size("dp")
    group_size = row_count // senders
    flattened = latents.reshape(row_count * frame_count, feature_width)
    drive = jnp.dot(
        flattened,
        lax.all_gather(w_in, "dp", axis=1, tiled=True),
        preferred_element_type=jnp.float32,
    ).reshape(row_count, frame_count, feature_width)
    narrow = jnp.dot(flattened, w_down, preferred_element_type=jnp.float32).astype(jnp.bfloat16)
    stride = jax.nn.softplus(jnp.dot(narrow, w_up, preferred_element_type=jnp.float32))
    decay = jnp.exp(-rate[None, :] * stride).reshape(row_count, frame_count, feature_width)
    first_frame = lax.axis_index("tm") * frame_count
    frame_ids = first_frame + jnp.arange(frame_count, dtype=jnp.int32)
    valid = (frame_ids[None, :] < lengths[:, None]).astype(jnp.float32)
    running = jnp.zeros((row_count, feature_width), jnp.float32)
    product_decay = jnp.ones((row_count, feature_width), jnp.float32)
    partial_states = []
    reaches = []
    for position in range(frame_count):
        running = (
            decay[:, position] * running + valid[:, position : position + 1] * drive[:, position]
        )
        product_decay = product_decay * decay[:, position]
        partial_states.append(running)
        reaches.append(product_decay)
    entering = jnp.zeros_like(running)
    leaving = running
    for position in range(lax.axis_size("tm") - 1):
        entering = passed_along(leaving, "tm", 1)
        leaving = product_decay * entering + running
    states = jnp.stack(
        [partial_value + reach * entering for partial_value, reach in zip(partial_states, reaches)],
        axis=1,
    )
    rounded = states.astype(jnp.bfloat16).reshape(row_count * frame_count, feature_width)
    mixed = flattened.astype(jnp.float32) + jnp.dot(
        rounded, lax.all_gather(w_out, "dp", axis=1, tiled=True), preferred_element_type=jnp.float32
    )
    scaling = lax.rsqrt(jnp.mean(mixed * mixed, axis=1, keepdims=True) + 1e-06)
    normed = (mixed * scaling * gain[None, :]).astype(jnp.bfloat16)
    logit_values = jnp.dot(normed, w_bits, preferred_element_type=jnp.float32)
    weight_mask = valid.reshape(row_count * frame_count, 1)
    chance = jax.nn.sigmoid(4.0 * logit_values)
    chance_sum, entropy_sum, commit_sum, count = lax.psum(
        (
            jnp.sum(chance * weight_mask, axis=0),
            jnp.sum(bit_entropy(logit_values) * weight_mask),
            jnp.sum(jnp.square(jnp.abs(logit_values) - 1.0) * weight_mask),
            jnp.sum(valid),
        ),
        ("dp", "tm"),
    )
    marginal = chance_sum / count
    batch_entropy = jnp.sum(
        -marginal * jnp.log(marginal) - (1.0 - marginal) * jnp.log(1.0 - marginal)
    )
    bit_count = logit_values.shape[1]
    slots = float(row_count * senders * frame_count * lax.axis_size("tm"))
    penalty = entropy_sum / slots - batch_entropy + 0.25 * commit_sum / slots
    coded = jnp.transpose(
        logit_values.astype(jnp.bfloat16).reshape(row_count, frame_count, bit_count), (2, 1, 0)
    )
    coded = lax.all_to_all(
        jnp.take(coded, plan, axis=2).reshape(bit_count, frame_count, senders, group_size),
        "dp",
        split_axis=2,
        concat_axis=2,
        tiled=True,
    ).reshape(bit_count, frame_count, row_count)
    return (coded, penalty)


def solution(mesh):
    return jax.shard_map(
        shards,
        mesh=mesh,
        in_specs=(
            P("dp", "tm", None),
            P("dp"),
            P("dp"),
            P(None, "dp"),
            P(),
            P(),
            P(None, "dp"),
            P(),
            P(),
            P(),
        ),
        out_specs=(P(None, "tm", "dp"), P()),
        check_vma=False,
    )
```

profile of v0, /device:TPU:1, one launch (start us, length us, event | category | flops | bytes accessed | tf_op | source)
XLA Modules:
  0.0 409.2 jit_solution(11331771406500634538)
XLA Ops:
  7.2 0.7 all-gather.3.cloned.1.call-update
  8.0 5.6 %copy.32 = bf16[256,6,1024]{2,1,0:T(8,128)(2,1)} copy(bf16[256,6,1024]{2,0,1:T(8,128)(2,1)} %param.10) | data formatting | bytes 6291456 | tf_op args[0]
  13.6 4.9 %reshape.65 = bf16[1536,1024]{1,0:T(8,128)(2,1)S(1)} reshape(bf16[256,6,1024]{2,1,0:T(8,128)(2,1)} %copy.32) | data formatting | bytes 6291456 | tf_op jit(solution)/shard_map/reshape | solution.py:23
  18.6 7.8 %fusion.1 = f32[1536,1024]{1,0:T(8,128)} fusion(bf16[64,1024]{1,0:T(8,128)(2,1)S(1)} %copy-done, f32[1024]{0:T(1024)S(1)} %neg.23, bf16[1536,1024]{1,0:T(8,128)(2,1)S(1)} %reshape.65, bf16[1024,64]{0,1:T(8,128)(2,1)S(1)} %copy-done.25), kind=kOutput, calls=%fused_computation.3 | convolution fusion | flops 413761536 | bytes 9703424 | tf_op jit(solution)/shard_map/dot_general | solution.py:30
  26.4 7.9 %reshape.66 = f32[256,6,1024]{2,1,0:T(8,128)} reshape(f32[1536,1024]{1,0:T(8,128)} %fusion.1) | data formatting | bytes 12582912 | tf_op jit(solution)/shard_map/reshape | solution.py:31
  34.4 0.5 slice_reduce_fusion
  34.9 24.0 %fusion.50 = (f32[256,1,1024]{2,1,0:T(1,128)S(1)}, f32[256,1,1024]{2,1,0:T(1,128)}, f32[256,1,1024]{2,1,0:T(1,128)}, f32[256,1,1024]{2,1,0:T(1,128)}, f32[256,1,1024]{2,1,0:T(1,128)S(1)}, /*index=5*/f32[256,1,1024]{2,1,0:T(1,128)}) fusion(f32[256,6,1024]{2,1,0:T(8,128)} %reshape.66), kind=kLoop, calls=%fused_computation.94 | loop fusion | bytes 12582912 | tf_op jit(solution)/shard_map/slice | solution.py:43
  59.0 37.4 %all-gather.3.cloned.1.call-done = bf16[1024,1024]{0,1:T(8,128)(2,1)} async-done(((bf16[1024,16]{0,1:T(8,128)(2,1)}), bf16[1024,1024]{0,1:T(8,128)(2,1)}) %all-gather.3.cloned.1.call-update) | async-done | bytes 2097168 | tf_op jit(solution)/shard_map/all_gather | solution.py:26
  96.4 6.2 %fusion.3 = f32[256,6,1024]{2,0,1:T(8,128)S(1)} fusion(bf16[256,6,1024]{2,0,1:T(8,128)(2,1)} %param.10, bf16[1024,1024]{0,1:T(8,128)(2,1)} %all-gather.3.cloned.1.call-done), kind=kOutput, calls=%fused_computation.9 | convolution fusion | flops 3221225472 | bytes 11534336 | tf_op jit(solution)/shard_map/dot_general | solution.py:24
  102.6 3.6 fusion.6
  106.5 7.6 %collective-permute-start = (f32[256,1024]{1,0:T(8,128)S(1)}, f32[256,1024]{1,0:T(8,128)S(1)}, u32[]{:S(2)}, u32[]{:S(2)}) collective-permute-start(f32[256,1024]{1,0:T(8,128)S(1)} %get-tuple-element.22), channel_id=1, source_target_pairs={{0,1},{1,2},{2,3},{3,4},{4,5},{5,6},{6,7},{8,9},{9,10},{10,11},{11... | collective-permute-start | bytes 3145736 | tf_op jit(solution)/shard_map/ppermute | solution.py:10
  114.1 11.7 %collective-permute-done = f32[256,1024]{1,0:T(8,128)S(1)} collective-permute-done((f32[256,1024]{1,0:T(8,128)S(1)}, f32[256,1024]{1,0:T(8,128)S(1)}, u32[]{:S(2)}, u32[]{:S(2)}) %collective-permute-start) | collective-permute-done | bytes 1048608 | tf_op jit(solution)/shard_map/ppermute | solution.py:10
  125.8 4.0 multiply_add_fusion.5
  129.8 4.4 %collective-permute-start.1 = (f32[256,1024]{1,0:T(8,128)S(1)}, f32[256,1024]{1,0:T(8,128)S(1)}, u32[]{:S(2)}, u32[]{:S(2)}) collective-permute-start(f32[256,1024]{1,0:T(8,128)S(1)} %get-tuple-element.19), channel_id=1, source_target_pairs={{0,1},{1,2},{2,3},{3,4},{4,5},{5,6},{6,7},{8,9},{9,10},{10,11},{11... | collective-permute-start | bytes 3145736 | tf_op jit(solution)/shard_map/ppermute | solution.py:10
  134.2 11.7 %collective-permute-done.1 = f32[256,1024]{1,0:T(8,128)S(1)} collective-permute-done((f32[256,1024]{1,0:T(8,128)S(1)}, f32[256,1024]{1,0:T(8,128)S(1)}, u32[]{:S(2)}, u32[]{:S(2)}) %collective-permute-start.1) | collective-permute-done | bytes 1048608 | tf_op jit(solution)/shard_map/ppermute | solution.py:10
  146.2 4.4 %collective-permute-start.2 = (f32[256,1024]{1,0:T(8,128)S(1)}, f32[256,1024]{1,0:T(8,128)S(1)}, u32[]{:S(2)}, u32[]{:S(2)}) collective-permute-start(f32[256,1024]{1,0:T(8,128)S(1)} %multiply_add_fusion.4), channel_id=1, source_target_pairs={{0,1},{1,2},{2,3},{3,4},{4,5},{5,6},{6,7},{8,9},{9,10},{10,11},{11... | collective-permute-start | bytes 3145736 | tf_op jit(solution)/shard_map/ppermute | solution.py:10
  150.6 11.7 %collective-permute-done.2 = f32[256,1024]{1,0:T(8,128)S(1)} collective-permute-done((f32[256,1024]{1,0:T(8,128)S(1)}, f32[256,1024]{1,0:T(8,128)S(1)}, u32[]{:S(2)}, u32[]{:S(2)}) %collective-permute-start.2) | collective-permute-done | bytes 1048608 | tf_op jit(solution)/shard_map/ppermute | solution.py:10
  162.6 4.4 %collective-permute-start.3 = (f32[256,1024]{1,0:T(8,128)S(1)}, f32[256,1024]{1,0:T(8,128)S(1)}, u32[]{:S(2)}, u32[]{:S(2)}) collective-permute-start(f32[256,1024]{1,0:T(8,128)S(1)} %multiply_add_fusion.3), channel_id=1, source_target_pairs={{0,1},{1,2},{2,3},{3,4},{4,5},{5,6},{6,7},{8,9},{9,10},{10,11},{11... | collective-permute-start | bytes 3145736 | tf_op jit(solution)/shard_map/ppermute | solution.py:10
  167.0 11.7 %collective-permute-done.3 = f32[256,1024]{1,0:T(8,128)S(1)} collective-permute-done((f32[256,1024]{1,0:T(8,128)S(1)}, f32[256,1024]{1,0:T(8,128)S(1)}, u32[]{:S(2)}, u32[]{:S(2)}) %collective-permute-start.3) | collective-permute-done | bytes 1048608 | tf_op jit(solution)/shard_map/ppermute | solution.py:10
  179.0 4.4 %collective-permute-start.4 = (f32[256,1024]{1,0:T(8,128)S(1)}, f32[256,1024]{1,0:T(8,128)S(1)}, u32[]{:S(2)}, u32[]{:S(2)}) collective-permute-start(f32[256,1024]{1,0:T(8,128)S(1)} %multiply_add_fusion.2), channel_id=1, source_target_pairs={{0,1},{1,2},{2,3},{3,4},{4,5},{5,6},{6,7},{8,9},{9,10},{10,11},{11... | collective-permute-start | bytes 3145736 | tf_op jit(solution)/shard_map/ppermute | solution.py:10
  183.4 11.7 %collective-permute-done.4 = f32[256,1024]{1,0:T(8,128)S(1)} collective-permute-done((f32[256,1024]{1,0:T(8,128)S(1)}, f32[256,1024]{1,0:T(8,128)S(1)}, u32[]{:S(2)}, u32[]{:S(2)}) %collective-permute-start.4) | collective-permute-done | bytes 1048608 | tf_op jit(solution)/shard_map/ppermute | solution.py:10
  195.1 0.3 multiply_add_fusion.1
  195.4 4.4 %collective-permute-start.5 = (f32[256,1024]{1,0:T(8,128)S(1)}, f32[256,1024]{1,0:T(8,128)}, u32[]{:S(2)}, u32[]{:S(2)}) collective-permute-start(f32[256,1024]{1,0:T(8,128)S(1)} %multiply_add_fusion.1), channel_id=1, source_target_pairs={{0,1},{1,2},{2,3},{3,4},{4,5},{5,6},{6,7},{8,9},{9,10},{10,11},{11... | collective-permute-start | bytes 3145736 | tf_op jit(solution)/shard_map/ppermute | solution.py:10
  199.8 11.7 %collective-permute-done.5 = f32[256,1024]{1,0:T(8,128)} collective-permute-done((f32[256,1024]{1,0:T(8,128)S(1)}, f32[256,1024]{1,0:T(8,128)}, u32[]{:S(2)}, u32[]{:S(2)}) %collective-permute-start.5) | collective-permute-done | bytes 1048608 | tf_op jit(solution)/shard_map/ppermute | solution.py:10
  211.5 2.5 multiply_add_fusion
  214.0 4.5 %collective-permute-start.6 = (f32[256,1024]{1,0:T(8,128)}, f32[256,1024]{1,0:T(8,128)S(1)}, u32[]{:S(2)}, u32[]{:S(2)}) collective-permute-start(f32[256,1024]{1,0:T(8,128)} %multiply_add_fusion), channel_id=1, source_target_pairs={{0,1},{1,2},{2,3},{3,4},{4,5},{5,6},{6,7},{8,9},{9,10},{10,11},{11... | collective-permute-start | bytes 3145736 | tf_op jit(solution)/shard_map/ppermute | solution.py:10
  218.7 5.0 %copy.33 = bf16[1536,1024]{0,1:T(8,128)(2,1)} copy(bf16[1536,1024]{1,0:T(8,128)(2,1)} %copy-done.10) | data formatting | bytes 6291456 | tf_op jit(solution)/shard_map/reshape | solution.py:23
  223.8 0.8 fusion.41
  224.6 6.0 %collective-permute-done.6 = f32[256,1024]{1,0:T(8,128)S(1)} collective-permute-done((f32[256,1024]{1,0:T(8,128)}, f32[256,1024]{1,0:T(8,128)S(1)}, u32[]{:S(2)}, u32[]{:S(2)}) %collective-permute-start.6) | collective-permute-done | bytes 1048608 | tf_op jit(solution)/shard_map/ppermute | solution.py:10
  230.6 1.8 fusion.23
  232.4 0.5 fusion.25
  232.9 0.7 copy-done.9
  233.6 0.3 copy-done.18
  233.9 0.6 fusion.27
  234.9 0.9 copy-done.7
  235.8 0.3 copy-done.17
  236.1 0.4 fusion.31
  236.7 3.8 copy.40
  240.5 6.5 %convert_element_type.32 = bf16[1536,1024]{1,0:T(8,128)(2,1)} reshape(bf16[256,6,1024]{2,1,0:T(8,128)(2,1)} %copy.40) | data formatting | bytes 6291456 | tf_op jit(solution)/shard_map/convert_element_type | solution.py:55
  247.0 28.8 %all-gather.5.cloned.1.call-done = bf16[1024,1024]{0,1:T(8,128)(2,1)} async-done(((bf16[1024,16]{0,1:T(8,128)(2,1)}), bf16[1024,1024]{0,1:T(8,128)(2,1)}) %all-gather.5.cloned.1.call-update) | async-done | bytes 2097168 | tf_op jit(solution)/shard_map/all_gather | solution.py:57
  275.8 6.1 %multiply_reduce_fusion = (f32[1536]{0:T(1024)S(1)}, f32[1536,1024]{0,1:T(8,128)S(1)}) fusion(bf16[1536,1024]{0,1:T(8,128)(2,1)S(1)} %copy-done.11, bf16[1536,1024]{1,0:T(8,128)(2,1)} %convert_element_type.32, bf16[1024,1024]{0,1:T(8,128)(2,1)} %all-gather.5.cloned.1.call-done), kind=kOutput, calls=%fused_computation.5 | convolution fusion | flops 3227515392 | bytes 14686208 | tf_op jit(solution)/shard_map/dot_general | solution.py:56
  281.9 1.9 multiply_reduce_fusion.1
  284.2 0.8 gather_fusion
  285.3 0.9 reshape.86
  286.2 8.4 %all-to-all-start = ((bf16[64,2,216]{2,1,0:T(2,128)(2,1)}), bf16[64,2,216]{2,1,0:T(2,128)(2,1)S(1)}, u32[]{:S(2)}, u32[]{:S(2)}) async-start(bf16[64,2,216]{2,1,0:T(2,128)(2,1)} %reshape.86), calls=%async_computation | async-start | bytes 131072 | tf_op jit(solution)/shard_map/all_to_all | solution.py:83
  294.6 101.9 %all-reduce = (f32[]{:T(128)}, f32[18]{0:T(128)S(1)}, f32[]{:T(128)}, f32[]{:T(128)}) all-reduce(f32[]{:T(128)} %get-tuple-element.7, f32[18]{0:T(128)S(1)} %get-tuple-element.8, f32[]{:T(128)} %fusion.41, f32[]{:T(128)} %get-tuple-element.6), channel_id=1, replica_groups=mesh['dp'=64,'tm'=8] {'dp','tm'}, use_global_device_ids=true, to_apply=%region_2.3 | all-reduce | flops 21 | bytes 168 | tf_op jit(solution)/shard_map/psum | solution.py:64
  397.2 1.4 fusion.43
  400.3 0.9 copy.44
  (71 shorter events, 3.3 us)
Async XLA Ops:
  7.2 11.4 %copy-start = (bf16[64,1024]{1,0:T(8,128)(2,1)S(1)}, bf16[64,1024]{1,0:T(8,128)(2,1)}, u32[]{:S(2)}) copy-start(bf16[64,1024]{1,0:T(8,128)(2,1)} %param.15) | copy-start | bytes 393220
  7.2 89.2 %all-gather.3.cloned.1.call-start = ((), (), s32[]{:S(2)}) async-start(), calls=%async_computation.1 | async-start | bytes 2129920 | tf_op jit(solution)/shard_map/all_gather | solution.py:26
  7.9 267.8 %all-gather.5.cloned.1.call-start = ((), (), s32[]{:S(2)}) async-start(), calls=%async_computation.2 | async-start | bytes 2129920 | tf_op jit(solution)/shard_map/all_gather | solution.py:57
  13.6 4.9 %copy-start.23 = (f32[1024]{0:T(1024)S(1)}, f32[1024]{0:T(1024)}, u32[]{:S(2)}) copy-start(f32[1024]{0:T(1024)} %param.17) | copy-start | bytes 12292
  13.6 5.0 %copy-start.25 = (bf16[1024,64]{0,1:T(8,128)(2,1)S(1)}, bf16[1024,64]{0,1:T(8,128)(2,1)}, u32[]{:S(2)}) copy-start(bf16[1024,64]{0,1:T(8,128)(2,1)} %param.14) | copy-start | bytes 393220
  18.5 7.9 %copy-start.10 = (bf16[1536,1024]{1,0:T(8,128)(2,1)}, bf16[1536,1024]{1,0:T(8,128)(2,1)S(1)}, u32[]{:S(2)}) copy-start(bf16[1536,1024]{1,0:T(8,128)(2,1)S(1)} %reshape.65) | copy-start | bytes 9437188
  26.4 7.9 %copy-start.22 = (s32[256]{0:T(256)S(1)}, s32[256]{0:T(256)}, u32[]{:S(2)}) copy-start(s32[256]{0:T(256)} %param.11) | copy-start | bytes 3076
  59.0 43.6 %copy-start.4 = (f32[256,1,1024]{2,1,0:T(1,128)}, f32[256,1,1024]{2,1,0:T(1,128)S(1)}, u32[]{:S(2)}) copy-start(f32[256,1,1024]{2,1,0:T(1,128)S(1)} %get-tuple-element.27) | copy-start | bytes 3145732
  59.0 66.9 %copy-start.2 = (f32[256,1,1024]{2,1,0:T(1,128)}, f32[256,1,1024]{2,1,0:T(1,128)S(1)}, u32[]{:S(2)}) copy-start(f32[256,1,1024]{2,1,0:T(1,128)S(1)} %get-tuple-element.31) | copy-start | bytes 3145732
  96.4 6.2 %copy-start.6 = (f32[256,1,1024]{2,1,0:T(1,128)S(1)}, f32[256,1,1024]{2,1,0:T(1,128)}, u32[]{:S(2)}) copy-start(f32[256,1,1024]{2,1,0:T(1,128)} %get-tuple-element.28) | copy-start | bytes 3145732
  96.4 6.2 %copy-start.8 = (f32[256,1,1024]{2,1,0:T(1,128)S(1)}, f32[256,1,1024]{2,1,0:T(1,128)}, u32[]{:S(2)}) copy-start(f32[256,1,1024]{2,1,0:T(1,128)} %get-tuple-element.30) | copy-start | bytes 3145732
  96.4 6.2 %copy-start.13 = (f32[256,1,1024]{2,1,0:T(1,128)S(1)}, f32[256,1,1024]{2,1,0:T(1,128)}, u32[]{:S(2)}) copy-start(f32[256,1,1024]{2,1,0:T(1,128)} %get-tuple-element.29) | copy-start | bytes 3145732
  96.4 6.2 %copy-start.14 = (f32[256,1,1024]{2,1,0:T(1,128)S(1)}, f32[256,1,1024]{2,1,0:T(1,128)}, u32[]{:S(2)}) copy-start(f32[256,1,1024]{2,1,0:T(1,128)} %get-tuple-element.32) | copy-start | bytes 3145732
  102.6 4.0 copy-start.15
  106.5 19.3 %collective-permute-start = (f32[256,1024]{1,0:T(8,128)S(1)}, f32[256,1024]{1,0:T(8,128)S(1)}, u32[]{:S(2)}, u32[]{:S(2)}) collective-permute-start(f32[256,1024]{1,0:T(8,128)S(1)} %get-tuple-element.22), channel_id=1, source_target_pairs={{0,1},{1,2},{2,3},{3,4},{4,5},{5,6},{6,7},{8,9},{9,10},{10,11},{11... | collective-permute-start | bytes 3145736 | tf_op jit(solution)/shard_map/ppermute | solution.py:10
  129.8 16.1 %collective-permute-start.1 = (f32[256,1024]{1,0:T(8,128)S(1)}, f32[256,1024]{1,0:T(8,128)S(1)}, u32[]{:S(2)}, u32[]{:S(2)}) collective-permute-start(f32[256,1024]{1,0:T(8,128)S(1)} %get-tuple-element.19), channel_id=1, source_target_pairs={{0,1},{1,2},{2,3},{3,4},{4,5},{5,6},{6,7},{8,9},{9,10},{10,11},{11... | collective-permute-start | bytes 3145736 | tf_op jit(solution)/shard_map/ppermute | solution.py:10
  146.2 16.1 %collective-permute-start.2 = (f32[256,1024]{1,0:T(8,128)S(1)}, f32[256,1024]{1,0:T(8,128)S(1)}, u32[]{:S(2)}, u32[]{:S(2)}) collective-permute-start(f32[256,1024]{1,0:T(8,128)S(1)} %multiply_add_fusion.4), channel_id=1, source_target_pairs={{0,1},{1,2},{2,3},{3,4},{4,5},{5,6},{6,7},{8,9},{9,10},{10,11},{11... | collective-permute-start | bytes 3145736 | tf_op jit(solution)/shard_map/ppermute | solution.py:10
  162.6 16.1 %collective-permute-start.3 = (f32[256,1024]{1,0:T(8,128)S(1)}, f32[256,1024]{1,0:T(8,128)S(1)}, u32[]{:S(2)}, u32[]{:S(2)}) collective-permute-start(f32[256,1024]{1,0:T(8,128)S(1)} %multiply_add_fusion.3), channel_id=1, source_target_pairs={{0,1},{1,2},{2,3},{3,4},{4,5},{5,6},{6,7},{8,9},{9,10},{10,11},{11... | collective-permute-start | bytes 3145736 | tf_op jit(solution)/shard_map/ppermute | solution.py:10
  179.0 16.1 %collective-permute-start.4 = (f32[256,1024]{1,0:T(8,128)S(1)}, f32[256,1024]{1,0:T(8,128)S(1)}, u32[]{:S(2)}, u32[]{:S(2)}) collective-permute-start(f32[256,1024]{1,0:T(8,128)S(1)} %multiply_add_fusion.2), channel_id=1, source_target_pairs={{0,1},{1,2},{2,3},{3,4},{4,5},{5,6},{6,7},{8,9},{9,10},{10,11},{11... | collective-permute-start | bytes 3145736 | tf_op jit(solution)/shard_map/ppermute | solution.py:10
  195.4 16.1 %collective-permute-start.5 = (f32[256,1024]{1,0:T(8,128)S(1)}, f32[256,1024]{1,0:T(8,128)}, u32[]{:S(2)}, u32[]{:S(2)}) collective-permute-start(f32[256,1024]{1,0:T(8,128)S(1)} %multiply_add_fusion.1), channel_id=1, source_target_pairs={{0,1},{1,2},{2,3},{3,4},{4,5},{5,6},{6,7},{8,9},{9,10},{10,11},{11... | collective-permute-start | bytes 3145736 | tf_op jit(solution)/shard_map/ppermute | solution.py:10
  214.0 16.5 %collective-permute-start.6 = (f32[256,1024]{1,0:T(8,128)}, f32[256,1024]{1,0:T(8,128)S(1)}, u32[]{:S(2)}, u32[]{:S(2)}) collective-permute-start(f32[256,1024]{1,0:T(8,128)} %multiply_add_fusion), channel_id=1, source_target_pairs={{0,1},{1,2},{2,3},{3,4},{4,5},{5,6},{6,7},{8,9},{9,10},{10,11},{11... | collective-permute-start | bytes 3145736 | tf_op jit(solution)/shard_map/ppermute | solution.py:10
  218.7 5.0 %copy-start.24 = (s32[256]{0:T(256)S(1)}, s32[256]{0:T(256)}, u32[]{:S(2)}) copy-start(s32[256]{0:T(256)} %param.12) | copy-start | bytes 3076
  223.8 8.7 %copy-start.3 = (f32[256,1,1024]{2,1,0:T(1,128)S(1)}, f32[256,1,1024]{2,1,0:T(1,128)}, u32[]{:S(2)}) copy-start(f32[256,1,1024]{2,1,0:T(1,128)} %copy-done.2) | copy-start | bytes 3145732
  223.8 8.7 %copy-start.5 = (f32[256,1,1024]{2,1,0:T(1,128)S(1)}, f32[256,1,1024]{2,1,0:T(1,128)}, u32[]{:S(2)}) copy-start(f32[256,1,1024]{2,1,0:T(1,128)} %copy-done.4) | copy-start | bytes 3145732
  223.8 8.7 %copy-start.19 = (f32[256,1024]{1,0:T(8,128)S(1)}, f32[256,1024]{1,0:T(8,128)}, u32[]{:S(2)}) copy-start(f32[256,1024]{1,0:T(8,128)} %get-tuple-element.26) | copy-start | bytes 3145732
  232.4 1.2 copy-start.9
  232.4 1.5 copy-start.18
  232.9 1.7 copy-start.12
  232.9 1.8 copy-start.16
  234.5 1.3 copy-start.7
  234.5 1.6 copy-start.17
  240.5 35.3 %copy-start.11 = (bf16[1536,1024]{0,1:T(8,128)(2,1)S(1)}, bf16[1536,1024]{0,1:T(8,128)(2,1)}, u32[]{:S(2)}) copy-start(bf16[1536,1024]{0,1:T(8,128)(2,1)} %copy.33) | copy-start | bytes 9437188
  247.0 34.9 %copy-start.20 = (bf16[1024,18]{0,1:T(8,128)(2,1)S(1)}, bf16[1024,18]{0,1:T(8,128)(2,1)}, u32[]{:S(2)}) copy-start(bf16[1024,18]{0,1:T(8,128)(2,1)} %param.19) | copy-start | bytes 110596
  247.0 34.9 %copy-start.21 = (f32[1024]{0:T(1024)S(1)}, f32[1024]{0:T(1024)}, u32[]{:S(2)}) copy-start(f32[1024]{0:T(1024)} %param.18) | copy-start | bytes 12292
  281.9 119.3 %copy-start.1 = (bf16[64,1024]{1,0:T(8,128)(2,1)S(1)}, bf16[64,1024]{1,0:T(8,128)(2,1)}, u32[]{:S(2)}) copy-start(bf16[64,1024]{1,0:T(8,128)(2,1)} %param.15) | copy-start | bytes 393220
  286.2 113.6 %all-to-all-start = ((bf16[64,2,216]{2,1,0:T(2,128)(2,1)}), bf16[64,2,216]{2,1,0:T(2,128)(2,1)S(1)}, u32[]{:S(2)}, u32[]{:S(2)}) async-start(bf16[64,2,216]{2,1,0:T(2,128)(2,1)} %reshape.86), calls=%async_computation | async-start | bytes 131072 | tf_op jit(solution)/shard_map/all_to_all | solution.py:83
Sparse Core Ops, SparseCore 0:
  11.0 85.2 all-gather.2
  200.0 75.7 all-gather.4
where the time goes:
time: 410 us; the launch traced here: 409 us
  waiting for transfers between devices  143 us (35%)
  blocking collectives  102 us (25%)
  local copies, waits for them, and re-layouts  64.6 us (16%)
  starting transfers between devices  42.5 us (10%)
  matrix products  22 us (5%)
  between operations  17.6 us (4%)
  other arithmetic  17.4 us (4%)
    psum x1, blocking collectives, shards(): lax.psum((jnp.sum(chance * weight_mask, axis=0), jnp.sum(bit_entropy(logi...  102 us
    ppermute x7, waiting for transfers between devices, passed_along(): lax.ppermute(value, axis, [(source, source + steps) for source in range(i...  76.3 us
    all_gather x1, waiting for transfers between devices, shards(): lax.all_gather(w_in, 'dp', axis=1, tiled=True)  37.4 us
    ppermute x7, starting transfers between devices, passed_along(): lax.ppermute(value, axis, [(source, source + steps) for source in range(i...  34 us
    all_gather x1, waiting for transfers between devices, shards(): lax.all_gather(w_out, 'dp', axis=1, tiled=True)  28.8 us
    slice x1, local copies, waits for them, and re-layouts, shards(): product_decay = product_decay * decay[:, position]  24 us
    unnamed x56, local copies, waits for them, and re-layouts  10.5 us
    reshape x2, local copies, waits for them, and re-layouts, shards(): flattened = latents.reshape(row_count * frame_count, feature_width)  9.87 us
  transfers between devices with their start and end apart: 10, of which 9 were waited for; matrix products, arithmetic and copies ran while one was open for 18% of the time, Pallas kernels for 0%

commit v1 on v0

v1 whole, which is shorter than its diff:
```python
import functools
import math

import jax
import jax.numpy as jnp
from jax import lax
from jax.experimental import pallas as pl
from jax.experimental.pallas import tpu as pltpu
from jax.sharding import PartitionSpec as P

MESH = pl.DeviceIdType.MESH
GROUP = 4
LANES = 128
CHUNKS = 4
LOG2E = math.log2(math.e)


def nt(a, b):
    return lax.dot_general(a, b, (((1,), (1,)), ((), ())), preferred_element_type=jnp.float32)


def nn(a, b):
    return jnp.dot(a, b, preferred_element_type=jnp.float32)


def kernel(
    dp_count, tm_count, x_hbm, lengths_ref, plan_ref, win_ref, wdown_ref, wup_ref, wout_ref, rate_ref,
    gain_ref, wbits_ref, codes_ref, penalty_ref,
    x_ref, wt, narrow, dec, drv, reach, local, ent, leave, states, mixed, wb, onehot, pick, len_b,
    logits, sendbuf, recvbuf, tmbuf,
    x_sem, p1_send, p1_recv, ring_send, ring_recv, sib_send, sib_recv, chain_send, chain_recv,
    a2a_send, a2a_recv, tm_send, tm_recv,
):
    frames, rows, width = x_ref.shape
    n = math.isqrt(dp_count)
    half = width // 2
    block = width // dp_count
    part = rows // CHUNKS
    tile = min(256, width)
    tiles = width // tile
    bits = wbits_ref.shape[0]
    packed = bits * frames
    me = lax.axis_index("dp")
    tm = lax.axis_index("tm")
    y, z = me // n, me % n
    core = tm % 2
    major = y * (1 - core) + z * core
    minor = z * (1 - core) + y * core

    def dp_of(major_id, minor_id):
        return (major_id * n + minor_id) * (1 - core) + (minor_id * n + major_id) * core

    def on_core(make):
        pl.when(core == 0)(lambda: make(0))
        pl.when(core == 1)(lambda: make(1))

    right = dp_of((major + 1) % n, minor)
    left = dp_of((major + n - 1) % n, minor)
    sibling = tm + 1 - 2 * core

    x_copy = pltpu.make_async_copy(x_hbm, x_ref, x_sem)
    x_copy.start()

    barrier = pltpu.get_barrier_semaphore()
    for step in range(1, n):
        peer = dp_of(major, (minor + step) % n)
        pl.semaphore_signal(barrier, inc=1, device_id=(peer, tm), device_id_type=MESH)
    for peer in (left, right):
        pl.semaphore_signal(barrier, inc=1, device_id=(peer, tm), device_id_type=MESH)
    for step in range(1, tm_count):
        pl.semaphore_signal(
            barrier, inc=1, device_id=(me, (tm + step) % tm_count), device_id_type=MESH
        )

    for w, ref in enumerate((win_ref, wout_ref)):
        @pl.when(core == 0)
        def _():
            wt[w, 0, y, z] = ref[:, :half]

        @pl.when(core == 1)
        def _():
            wt[w, 1, y, z] = ref[:, half:]

    pl.semaphore_wait(barrier, (n - 1) + 2 + (tm_count - 1))

    def group(w, c, major_id, low=0, count=n):
        if c == 0:
            return wt.at[w, 0, major_id, pl.ds(low, count)]
        return wt.at[w, 1, pl.ds(low, count), major_id]

    for w in range(2):
        for step in range(1, n):
            pltpu.make_async_remote_copy(
                src_ref=wt.at[w, core, y, z], dst_ref=wt.at[w, core, y, z],
                send_sem=p1_send.at[w], recv_sem=p1_recv.at[w],
                device_id=(dp_of(major, (minor + step) % n), tm), device_id_type=MESH,
            ).start()

    def remote(ref, send, recv, device):
        return pltpu.make_async_remote_copy(
            src_ref=ref, dst_ref=ref, send_sem=send, recv_sem=recv,
            device_id=device, device_id_type=MESH,
        )

    def to_sibling(w, c, major_id, low=0, count=n):
        remote(
            group(w, c, major_id, low, count), sib_send.at[w], sib_recv.at[w], (me, sibling)
        ).start()

    last = n // 2

    def pieces(w, c, step, ahead):
        back = (major + n - (step - 1) - ahead) % n
        forth = (major + (step - 1) + ahead) % n
        if step < last:
            return group(w, c, back), group(w, c, forth)
        return group(w, c, back, 0, n // 2), group(w, c, forth, n // 2, n // 2)

    def ring_start(w, step):
        def make(c):
            rightward, leftward = pieces(w, c, step, 0)
            remote(
                rightward, ring_send.at[w, 0, step - 1], ring_recv.at[w, 0, step - 1], (right, tm)
            ).start()
            remote(
                leftward, ring_send.at[w, 1, step - 1], ring_recv.at[w, 1, step - 1], (left, tm)
            ).start()
        on_core(make)

    def ring_arrive(w, step):
        def make(c):
            rightward, leftward = pieces(w, c, step, 1)
            remote(
                rightward, ring_send.at[w, 0, step - 1], ring_recv.at[w, 0, step - 1], (right, tm)
            ).wait_recv()
            remote(
                leftward, ring_send.at[w, 1, step - 1], ring_recv.at[w, 1, step - 1], (left, tm)
            ).wait_recv()
            for piece in (rightward, leftward):
                remote(piece, sib_send.at[w], sib_recv.at[w], (me, sibling)).start()
        on_core(make)

    def ring_sent(w, step):
        def make(c):
            rightward, leftward = pieces(w, c, step, 0)
            remote(
                rightward, ring_send.at[w, 0, step - 1], ring_recv.at[w, 0, step - 1], (right, tm)
            ).wait_send()
            remote(
                leftward, ring_send.at[w, 1, step - 1], ring_recv.at[w, 1, step - 1], (left, tm)
            ).wait_send()
        on_core(make)

    def first_arrive(w):
        def make(c):
            remote(
                group(w, c, major, 0, n - 1), p1_send.at[w], p1_recv.at[w], (right, tm)
            ).wait_recv()
            to_sibling(w, c, major)
        on_core(make)

    def small_things():
        first = tm * frames
        lengths = jnp.broadcast_to(lengths_ref[...].astype(jnp.float32), (LANES, rows))
        len_b[...] = lengths.T - first.astype(jnp.float32)
        spread = dp_count * 8
        slot = lax.broadcasted_iota(jnp.int32, (rows, spread), 1)
        source = lax.broadcasted_iota(jnp.int32, (rows, spread), 0)
        kept = slot % 8 < GROUP
        expand = jnp.where(kept & ((slot // 8) * GROUP + slot % 8 == source), 1.0, 0.0)
        expand = expand.astype(jnp.bfloat16)
        pick[...] = expand.T
        plan_rows = jnp.broadcast_to(plan_ref[...].astype(jnp.float32), (8, rows))
        wanted = nn(plan_rows.astype(jnp.bfloat16), expand)[0:1]
        chosen = jnp.where(kept & (wanted == source.astype(jnp.float32)), 1.0, 0.0)
        onehot[...] = chosen.T.astype(jnp.bfloat16)

    def spread_bits():
        place = lax.broadcasted_iota(jnp.int32, (LANES, bits), 0)
        bit = lax.broadcasted_iota(jnp.int32, (LANES, bits), 1)
        for t in range(frames):
            chooser = jnp.where(place == bit * frames + t, 1.0, 0.0).astype(jnp.bfloat16)
            wb[t] = nn(chooser, wbits_ref[...]).astype(jnp.bfloat16)

    def narrowing():
        x_copy.wait()
        for t in range(frames):
            narrow[t] = nt(x_ref[t], wdown_ref[...]).astype(jnp.bfloat16)

    def decays(t):
        for i in range(tiles):
            cols = slice(i * tile, (i + 1) * tile)
            u = nn(narrow[t], wup_ref[:, cols]) * LOG2E
            soft = jnp.maximum(u, 0.0) + jnp.log2(1.0 + jnp.exp2(-jnp.abs(u)))
            d = jnp.exp2(-rate_ref[:, cols] * soft)
            dec[t, :, cols] = d
            reach[:, cols] = d if t == 0 else reach[:, cols] * d

    def late(step):
        if step < frames:
            decays(step)

    narrowing()
    first_arrive(0)
    ring_start(0, 1)
    first_arrive(1)
    ring_start(1, 1)
    done = 0
    for step in range(1, last + 1):
        late(done)
        done += 1
        ring_arrive(0, step)
        if step < last:
            ring_start(0, step + 1)
        ring_arrive(1, step)
        if step < last:
            ring_start(1, step + 1)
    small_things()
    spread_bits()
    while done < frames:
        late(done)
        done += 1

    def sibling_arrived(w):
        theirs = wt.at[w, 1 - core]
        remote(theirs, sib_send.at[w], sib_recv.at[w], (me, sibling)).wait_recv()

    def weight_rows(w, i):
        per = n // tiles
        both = [wt[w, c, i * per:(i + 1) * per].reshape(tile, half) for c in range(2)]
        return jnp.concatenate(both, axis=1)

    @pl.when(tm == 0)
    def _():
        ent[...] = jnp.zeros_like(ent)

    def valid_of(k, t):
        rs = slice(k * part, (k + 1) * part)
        return jnp.where(len_b[rs, :] > float(t), 1.0, 0.0)

    def drives(k):
        rs = slice(k * part, (k + 1) * part)
        left_side = x_ref[:, rs, :].reshape(frames * part, width)
        for i in range(tiles):
            cols = slice(i * tile, (i + 1) * tile)
            pushed = nt(left_side, weight_rows(0, i)).reshape(frames, part, tile)
            running = None
            for t in range(frames):
                mask = jnp.concatenate([valid_of(k, t)] * max(1, tile // LANES), axis=1)[:, :tile]
                now = pushed[t] * mask
                drv[t, rs, cols] = now
                running = now if t == 0 else dec[t, rs, cols] * running + now
            local[rs, cols] = running

    def pass_on(k):
        rs = slice(k * part, (k + 1) * part)

        @pl.when(tm > 0)
        def _():
            remote(ent.at[k], chain_send.at[k], chain_recv.at[k], (me, tm)).wait_recv()

        @pl.when(tm < tm_count - 1)
        def _():
            out = reach[rs, :] * ent[k].astype(jnp.float32) + local[rs, :]
            leave[k] = out.astype(jnp.bfloat16)
            pltpu.make_async_remote_copy(
                src_ref=leave.at[k], dst_ref=ent.at[k],
                send_sem=chain_send.at[k], recv_sem=chain_recv.at[k],
                device_id=(me, (tm + 1) % tm_count), device_id_type=MESH,
            ).start()

    def outputs(k):
        rs = slice(k * part, (k + 1) * part)
        for i in range(tiles):
            cols = slice(i * tile, (i + 1) * tile)
            s = ent[k, :, cols].astype(jnp.float32)
            for t in range(frames):
                s = dec[t, rs, cols] * s + drv[t, rs, cols]
                states[t, :, cols] = s.astype(jnp.bfloat16)
        left_side = states[...].reshape(frames * part, width)
        square = None
        for i in range(tiles):
            cols = slice(i * tile, (i + 1) * tile)
            x = x_ref[:, rs, cols].reshape(frames * part, tile).astype(jnp.float32)
            m = x + nt(left_side, weight_rows(1, i))
            mixed[:, cols] = m
            square = m * m if i == 0 else square + m * m
        scaling = lax.rsqrt(jnp.sum(square, axis=1, keepdims=True) * (1.0 / width) + 1e-06)
        total = None
        for t in range(frames):
            ts = slice(t * part, (t + 1) * part)
            normed = (mixed[ts, :] * scaling[ts, :] * gain_ref[...]).astype(jnp.bfloat16)
            term = nt(normed, wb[t])
            total = term if t == 0 else total + term
        logits[rs, :] = total

    sibling_arrived(0)
    drives(0)
    pass_on_order = []
    for k in range(CHUNKS):
        if k + 1 < CHUNKS:
            drives(k + 1)
        pass_on(k)
        if k == 0:
            sibling_arrived(1)
        outputs(k)

    values = logits[...]
    lane = lax.broadcasted_iota(jnp.int32, (rows, LANES), 1)
    frame = (lane % frames).astype(jnp.float32)
    weight = jnp.where((len_b[...] > frame) & (lane < packed), 1.0, 0.0)
    scaled = 4.0 * values
    size = jnp.abs(scaled)
    e = jnp.exp(-size)
    inverse = 1.0 / (1.0 + e)
    chance = jnp.where(scaled >= 0.0, inverse, e * inverse)
    entropy = jnp.log(1.0 + e) + size * e * inverse
    commit = jnp.square(jnp.abs(values) - 1.0)

    def summed(value):
        return jnp.sum(value * weight, axis=0, keepdims=True)

    row8 = lax.broadcasted_iota(jnp.int32, (8, LANES), 0)
    sums = jnp.zeros((8, LANES), jnp.float32)
    for row, value in enumerate((chance, entropy, commit, jnp.ones_like(weight))):
        sums = jnp.where(row8 == GROUP + row, summed(value), sums)

    dealt = nn(onehot[...], values.astype(jnp.bfloat16))
    sendbuf[...] = dealt.reshape(dp_count, 8, LANES) + sums[None]
    recvbuf[me] = sendbuf[me]

    def deal(step, carry):
        peer = (me + step) % dp_count
        pltpu.make_async_remote_copy(
            src_ref=sendbuf.at[peer], dst_ref=recvbuf.at[me], send_sem=a2a_send, recv_sem=a2a_recv,
            device_id=(peer, tm), device_id_type=MESH,
        ).start()
        return carry

    lax.fori_loop(1, dp_count, deal, 0)
    arrived = recvbuf.at[pl.ds(0, dp_count - 1)]
    remote(arrived, a2a_send, a2a_recv, (right, tm)).wait_recv()

    tmbuf[tm] = jnp.sum(recvbuf[...], axis=0)
    for step in range(1, tm_count):
        remote(tmbuf.at[tm], tm_send, tm_recv, (me, (tm + step) % tm_count)).start()

    turned = recvbuf[...].reshape(dp_count * 8, LANES).T.astype(jnp.bfloat16)
    placed = nn(turned, pick[...])
    for b in range(bits):
        codes_ref[b] = placed[b * frames:(b + 1) * frames, :].astype(jnp.bfloat16)

    remote(
        tmbuf.at[pl.ds(0, tm_count - 1)], tm_send, tm_recv, (me, sibling)
    ).wait_recv()
    totals = tmbuf[0]
    for i in range(1, tm_count):
        totals = totals + tmbuf[i]
    lane1 = lax.broadcasted_iota(jnp.int32, (1, LANES), 1)
    chance_row = totals[GROUP:GROUP + 1, :]
    folded = chance_row
    for t in range(1, frames):
        folded = folded + pltpu.roll(chance_row, LANES - t, axis=1)
    count = jnp.sum(jnp.where(lane1 < frames, totals[GROUP + 3:GROUP + 4, :], 0.0))
    is_bit = (lane1 % frames == 0) & (lane1 < packed)
    marginal = jnp.where(is_bit, folded, 0.5 * count) / count
    terms = -marginal * jnp.log(marginal) - (1.0 - marginal) * jnp.log(1.0 - marginal)
    batch_entropy = jnp.sum(jnp.where(is_bit, terms, 0.0))
    entropy_sum = jnp.sum(totals[GROUP + 1:GROUP + 2, :])
    commit_sum = jnp.sum(totals[GROUP + 2:GROUP + 3, :])
    slots = 1.0 / float(rows * dp_count * frames * tm_count)
    penalty_ref[0, 0] = entropy_sum * slots - batch_entropy + 0.25 * commit_sum * slots

    for w in range(2):
        def first_sent(c, w=w):
            remote(
                group(w, c, major, 0, n - 1), p1_send.at[w], p1_recv.at[w], (right, tm)
            ).wait_send()
        on_core(first_sent)
        for step in range(1, last + 1):
            ring_sent(w, step)
        remote(wt.at[w, core], sib_send.at[w], sib_recv.at[w], (me, sibling)).wait_send()

    @pl.when(tm < tm_count - 1)
    def _():
        for k in range(CHUNKS):
            remote(leave.at[k], chain_send.at[k], chain_recv.at[k], (me, sibling)).wait_send()

    remote(arrived, a2a_send, a2a_recv, (right, tm)).wait_send()
    remote(
        tmbuf.at[pl.ds(0, tm_count - 1)], tm_send, tm_recv, (me, sibling)
    ).wait_send()


def shards(latents, lengths, plan, w_in, w_down, w_up, w_out, rate, gain, w_bits):
    rows, frames, width = latents.shape
    dp_count, tm_count = lax.axis_size("dp"), lax.axis_size("tm")
    n = math.isqrt(dp_count)
    bits = w_bits.shape[1]
    narrow_width = w_down.shape[1]
    part = rows // CHUNKS
    block = width // dp_count
    steps = n // 2
    vmem = pl.BlockSpec(memory_space=pltpu.VMEM)
    bf16, f32 = jnp.bfloat16, jnp.float32
    dma = pltpu.SemaphoreType.DMA
    codes, penalty = pl.pallas_call(
        functools.partial(kernel, dp_count, tm_count),
        out_shape=(
            jax.ShapeDtypeStruct((bits, frames, rows), bf16),
            jax.ShapeDtypeStruct((1, 1), f32),
        ),
        in_specs=[pl.BlockSpec(memory_space=pl.ANY)] + [vmem] * 9,
        out_specs=(vmem, pl.BlockSpec(memory_space=pltpu.SMEM)),
        scratch_shapes=[
            pltpu.VMEM((frames, rows, width), bf16),
            pltpu.VMEM((2, 2, n, n, block, width // 2), bf16),
            pltpu.VMEM((frames, rows, narrow_width), bf16),
            pltpu.VMEM((frames, rows, width), f32),
            pltpu.VMEM((frames, rows, width), f32),
            pltpu.VMEM((rows, width), f32),
            pltpu.VMEM((rows, width), f32),
            pltpu.VMEM((CHUNKS, part, width), bf16),
            pltpu.VMEM((CHUNKS, part, width), bf16),
            pltpu.VMEM((frames, part, width), bf16),
            pltpu.VMEM((frames * part, width), f32),
            pltpu.VMEM((frames, LANES, width), bf16),
            pltpu.VMEM((dp_count * 8, rows), bf16),
            pltpu.VMEM((dp_count * 8, rows), bf16),
            pltpu.VMEM((rows, LANES), f32),
            pltpu.VMEM((rows, LANES), f32),
            pltpu.VMEM((dp_count, 8, LANES), f32),
            pltpu.VMEM((dp_count, 8, LANES), f32),
            pltpu.VMEM((tm_count, 8, LANES), f32),
            dma,
            dma((2,)), dma((2,)),
            dma((2, 2, steps)), dma((2, 2, steps)),
            dma((2,)), dma((2,)),
            dma((CHUNKS,)), dma((CHUNKS,)),
            dma, dma, dma, dma,
        ],
        compiler_params=pltpu.CompilerParams(
            collective_id=0, has_side_effects=True, vmem_limit_bytes=56 * 1024 * 1024
        ),
    )(
        jnp.transpose(latents, (1, 0, 2)), lengths.reshape(1, rows), plan.reshape(1, rows),
        w_in.T, w_down.T, w_up, w_out.T, rate.reshape(1, width), gain.reshape(1, width), w_bits.T,
    )
    return codes, penalty[0, 0]


def solution(mesh):
    return jax.shard_map(
        shards,
        mesh=mesh,
        in_specs=(
            P("dp", "tm", None),
            P("dp"),
            P("dp"),
            P(None, "dp"),
            P(),
            P(),
            P(None, "dp"),
            P(),
            P(),
            P(),
        ),
        out_specs=(P(None, "tm", "dp"), P()),
        check_vma=False,
    )
```

time: 410 us -> 87.8 us (0.21)
  waiting for transfers between devices: 143 us -> 0 us
  blocking collectives: 102 us -> 0 us
  Pallas kernels: 0 us -> 83.7 us
  local copies, waits for them, and re-layouts: 64.6 us -> 1.52 us
  starting transfers between devices: 42.5 us -> 0 us
  matrix products: 22 us -> 0 us
  other arithmetic: 17.4 us -> 0 us
  between operations: 17.6 us -> 2.33 us
    psum x1 -> x0, blocking collectives: 102 us -> none  [shards(): lax.psum((jnp.sum(chance * weight_mask, axis=0), jnp.sum(bit_entropy(logi...]
    pallas_call x0 -> x1, Pallas kernels: none -> 83.7 us  [shards(): pl.pallas_call(functools.partial(kernel, dp_count, tm_count), out_shape=(...]
    ppermute x7 -> x0, waiting for transfers between devices: 76.3 us -> none  [passed_along(): lax.ppermute(value, axis, [(source, source + steps) for source in range(i...]
    all_gather x2 -> x0, waiting for transfers between devices: 66.2 us -> none  [the longest x1 37.4 us: shards(): lax.all_gather(w_in, 'dp', axis=1, tiled=True)]
    ppermute x7 -> x0, starting transfers between devices: 34 us -> none  [passed_along(): lax.ppermute(value, axis, [(source, source + steps) for source in range(i...]
    slice x2 -> x0, local copies, waits for them, and re-layouts: 24.5 us -> none  [the longest x1 24 us: shards(): product_decay = product_decay * decay[:, position]]
    dot_general x4 -> x0, matrix products: 22 us -> none  [the longest x1 7.81 us: shards(): jnp.dot(narrow, w_up, preferred_element_type=jnp.float32)]
    reshape x4 -> x0, local copies, waits for them, and re-layouts: 17.9 us -> none  [the longest x2 9.87 us: shards(): flattened = latents.reshape(row_count * frame_count, feature_width)]
  transfers between devices with their start and end apart: 10 -> 0, of which waited for: 9 -> 0; matrix products, arithmetic and copies ran while one was open for 18% -> 0% of each run, Pallas kernels for 0% -> 0%
where the time goes in v1:
time: 87.8 us; the launch traced here: 87.6 us
  Pallas kernels  83.7 us (95%)
  between operations  2.33 us (3%)
  local copies, waits for them, and re-layouts  1.52 us (2%)
    pallas_call x1, Pallas kernels, shards(): pl.pallas_call(functools.partial(kernel, dp_count, tm_count), out_shape=(...  83.7 us

profile of v1, /device:TPU:1, one launch (start us, length us, event | category | flops | bytes accessed | tf_op | source)
XLA Modules:
  0.0 87.6 jit_solution(11660951740657179343)
XLA Ops:
  0.6 83.7 %shard_map.113 = (bf16[18,6,256]{2,1,0:T(8,128)(2,1)}, f32[1,1]{1,0:T(1,128)}) custom-call(bf16[6,256,1024]{2,1,0:T(8,128)(2,1)} %bitcast.10, s32[1,256]{1,0:T(1,128)} %bitcast.17, s32[1,256]{1,0:T(1,128)} %bitcast.18, bf16[16,1024]{1,0:T(8,128)(2,1)} %bitcast.13, bf16[64,1024]{1,0:T(8,128)(2,1)} %bitcast.11, bf16[64,1024]{1,0:T(8,128)(2,1)} %wup_ref.1, ...), custom_call_target="tpu_custom_call" | custom-call | tf_op jit(solution)/shard_map/pallas_call | solution.py:407
  84.4 1.5 %copy.14 = bf16[18,6,256]{2,1,0:T(8,128)(2,1)} copy(bf16[18,6,256]{2,1,0:T(8,128)(2,1)} %get-tuple-element.8) | data formatting | bytes 110592

commit v2 on v1

v2 whole, which is shorter than its diff:
```python
import functools
import math

import jax
import jax.numpy as jnp
from jax import lax
from jax.experimental import pallas as pl
from jax.experimental.pallas import tpu as pltpu
from jax.sharding import PartitionSpec as P

MESH = pl.DeviceIdType.MESH
GROUP = 4
LANES = 128
CHUNKS = 4
PIECES = 8
LOG2E = math.log2(math.e)


def nt(a, b):
    return lax.dot_general(a, b, (((1,), (1,)), ((), ())), preferred_element_type=jnp.float32)


def nn(a, b):
    return jnp.dot(a, b, preferred_element_type=jnp.float32)


def kernel(
    dp_count, tm_count, x_hbm, lengths_ref, plan_ref, win_ref, wdown_ref, wup_ref, wout_ref, rate_ref,
    gain_ref, wbits_ref, codes_ref, penalty_ref,
    x_ref, wt, narrow, dec, drv, reach, local, reach0, local0, ent, leave, enter, states, mixed, wb,
    onehot, pick, len_b, logits, sums, sendbuf, recvbuf, tmbuf,
    x_sem, p1_send, p1_recv, p2_send, p2_recv, xs_send, xs_recv, sib_send, sib_recv,
    reach_send, reach_recv, local_send, local_recv, chain_send, chain_recv, fwd_send,
    a2a_send, a2a_recv, tm_send, tm_recv,
):
    frames, rows, width = x_ref.shape
    n = math.isqrt(dp_count)
    quarter = width // 4
    part = rows // CHUNKS
    piece = rows // PIECES
    per_chunk = PIECES // CHUNKS
    tile = min(256, width)
    tiles = width // tile
    bits = wbits_ref.shape[0]
    packed = bits * frames
    chips = tm_count // 2
    me = lax.axis_index("dp")
    tm = lax.axis_index("tm")
    y, z = me // n, me % n
    chip, core = tm // 2, tm % 2
    odd = chip % 2
    major = y * (1 - core) + z * core
    minor = z * (1 - core) + y * core
    mine = 2 * core + odd
    other = 2 * core + 1 - odd
    sibling = tm + 1 - 2 * core
    next_chip = ((chip + 1) % chips) * 2 + core
    last_chip = ((chip + chips - 1) % chips) * 2 + core

    def dp_of(major_id, minor_id):
        return (major_id * n + minor_id) * (1 - core) + (minor_id * n + major_id) * core

    def on_core(make):
        pl.when(core == 0)(lambda: make(0))
        pl.when(core == 1)(lambda: make(1))

    offsets = [o for step in range(1, n // 2) for o in (step, -step)] + [n // 2]

    x_copy = pltpu.make_async_copy(x_hbm, x_ref, x_sem)
    x_copy.start()
    recvbuf[...] = jnp.zeros_like(recvbuf)

    barrier = pltpu.get_barrier_semaphore()

    def greet(dp_id, tm_id):
        pl.semaphore_signal(barrier, inc=1, device_id=(dp_id, tm_id), device_id_type=MESH)

    for step in range(1, n):
        greet(dp_of(major, (minor + step) % n), tm)
    for step in range(1, n):
        greet(dp_of((major + step) % n, minor), tm)
    for step in range(1, tm_count):
        greet(me, (tm + step) % tm_count)

    wt[0, mine, y, z] = win_ref[:, pl.ds(pl.multiple_of(mine * quarter, quarter), quarter)]
    for i in range(2):
        start = pl.multiple_of((2 * core + i) * quarter, quarter)
        wt[1, 2 * core + i, y, z] = wout_ref[:, pl.ds(start, quarter)]

    @pl.when(chip == 0)
    def _():
        ent[...] = jnp.zeros_like(ent)

    pl.semaphore_wait(barrier, 2 * (n - 1) + (tm_count - 1))

    def remote(ref, send, recv, device):
        return pltpu.make_async_remote_copy(
            src_ref=ref, dst_ref=ref, send_sem=send, recv_sem=recv,
            device_id=device, device_id_type=MESH,
        )

    firsts, counts = (mine, 2 * core), (1, 2)

    def group(w, c, major_id, first=None, low=0, count=n):
        quarters = pl.ds(firsts[w] if first is None else first, counts[w])
        if c == 0:
            return wt.at[w, quarters, major_id, pl.ds(low, count)]
        return wt.at[w, quarters, pl.ds(low, count), major_id]

    def group_id(position):
        return major if position == 0 else (major + 2 * n - offsets[position - 1]) % n

    def p1_start(w):
        for step in range(1, n):
            remote(
                wt.at[w, pl.ds(firsts[w], counts[w]), y, z], p1_send.at[w], p1_recv.at[w],
                (dp_of(major, (minor + step) % n), tm),
            ).start()

    def p1_all(w, c):
        return remote(
            group(w, c, major, None, 0, n - 1), p1_send.at[w], p1_recv.at[w], (me, sibling)
        )

    def p2_start(w):
        def make(c):
            p1_all(w, c).wait_recv()
            for i, offset in enumerate(offsets):
                remote(
                    group(w, c, major), p2_send.at[w], p2_recv.at[w, i],
                    (dp_of((major + offset + n) % n, minor), tm),
                ).start()
            forward(w, c, 0)
        on_core(make)

    def forward(w, c, position):
        held = group(w, c, group_id(position))
        if w == 0:
            target = next_chip if position % 2 == 0 else last_chip
            remote(held, xs_send, xs_recv.at[position], (me, target)).start()
        remote(held, sib_send.at[w], sib_recv.at[w], (me, sibling)).start()

    def p2_arrive(w, position):
        def make(c):
            remote(
                group(w, c, group_id(position)), p2_send.at[w], p2_recv.at[w, position - 1],
                (me, sibling),
            ).wait_recv()
            forward(w, c, position)
        on_core(make)

    def x_arrive(position):
        def make(c):
            held = group(0, c, group_id(position), other)
            remote(held, xs_send, xs_recv.at[position], (me, sibling)).wait_recv()
            remote(held, sib_send.at[0], sib_recv.at[0], (me, sibling)).start()
        on_core(make)

    def sibling_arrived(w):
        theirs = wt.at[w, pl.ds(2 * (1 - core), 2)]
        remote(theirs, sib_send.at[w], sib_recv.at[w], (me, sibling)).wait_recv()

    def small_things():
        first = tm * frames
        lengths = jnp.broadcast_to(lengths_ref[...].astype(jnp.float32), (LANES, rows))
        len_b[...] = lengths.T - first.astype(jnp.float32)
        spread = dp_count * 8
        slot = lax.broadcasted_iota(jnp.int32, (rows, spread), 1)
        source = lax.broadcasted_iota(jnp.int32, (rows, spread), 0)
        kept = slot % 8 < GROUP
        expand = jnp.where(kept & ((slot // 8) * GROUP + slot % 8 == source), 1.0, 0.0)
        expand = expand.astype(jnp.bfloat16)
        pick[...] = expand.T
        plan_rows = jnp.broadcast_to(plan_ref[...].astype(jnp.float32), (8, rows))
        wanted = nn(plan_rows.astype(jnp.bfloat16), expand)[0:1]
        chosen = jnp.where(kept & (wanted == source.astype(jnp.float32)), 1.0, 0.0)
        onehot[...] = chosen.T.astype(jnp.bfloat16)
        place = lax.broadcasted_iota(jnp.int32, (LANES, bits), 0)
        bit = lax.broadcasted_iota(jnp.int32, (LANES, bits), 1)
        for t in range(frames):
            chooser = jnp.where(place == bit + t * bits, 1.0, 0.0).astype(jnp.bfloat16)
            wb[t] = nn(chooser, wbits_ref[...]).astype(jnp.bfloat16)
        sums[...] = jnp.zeros_like(sums)

    def narrowing():
        x_copy.wait()
        for t in range(frames):
            narrow[t] = nt(x_ref[t], wdown_ref[...]).astype(jnp.bfloat16)

    def decays(t):
        for i in range(tiles):
            cols = slice(i * tile, (i + 1) * tile)
            u = nn(narrow[t], wup_ref[:, cols]) * LOG2E
            soft = jnp.maximum(u, 0.0) + jnp.log2(1.0 + jnp.exp2(-jnp.abs(u)))
            d = jnp.exp2(-rate_ref[:, cols] * soft)
            dec[t, :, cols] = d
            reach[:, cols] = d if t == 0 else reach[:, cols] * d

    def decay_frames(low, high):
        for t in range(low, min(high, frames)):
            decays(t)

    positions = len(offsets) + 1
    p1_start(0)
    narrowing()
    decay_frames(0, 1)
    p2_start(0)
    decay_frames(1, 3)
    x_done = 0
    for position in range(1, positions):
        p2_arrive(0, position)
        if position == 1:
            p1_start(1)
        if position == positions - 2 or positions == 2:
            p2_start(1)
        if position >= 4:
            x_arrive(x_done)
            x_done += 1
        if position == min(4, positions - 1):
            decay_frames(3, 4)
    decay_frames(4, 5)
    while x_done < positions - 2:
        x_arrive(x_done)
        x_done += 1
    decay_frames(5, frames)

    @pl.when(core == 0)
    def _():
        pltpu.make_async_remote_copy(
            src_ref=reach, dst_ref=reach0, send_sem=reach_send, recv_sem=reach_recv,
            device_id=(me, sibling), device_id_type=MESH,
        ).start()

    small_things()
    while x_done < positions:
        x_arrive(x_done)
        x_done += 1

    def weight_rows(w, i):
        per = n // tiles
        all_quarters = [wt[w, q, i * per:(i + 1) * per].reshape(tile, quarter) for q in range(4)]
        return jnp.concatenate(all_quarters, axis=1)

    def valid_of(k, t):
        rs = slice(k * part, (k + 1) * part)
        return jnp.where(len_b[rs, :] > float(t), 1.0, 0.0)

    def drives(k):
        rs = slice(k * part, (k + 1) * part)
        left_side = x_ref[:, rs, :].reshape(frames * part, width)
        for i in range(tiles):
            cols = slice(i * tile, (i + 1) * tile)
            pushed = nt(left_side, weight_rows(0, i)).reshape(frames, part, tile)
            running = None
            for t in range(frames):
                mask = jnp.concatenate([valid_of(k, t)] * max(1, tile // LANES), axis=1)[:, :tile]
                now = pushed[t] * mask
                drv[t, rs, cols] = now
                running = now if t == 0 else dec[t, rs, cols] * running + now
            local[rs, cols] = running

        @pl.when(core == 0)
        def _():
            pltpu.make_async_remote_copy(
                src_ref=local.at[pl.ds(k * part, part)], dst_ref=local0.at[pl.ds(k * part, part)],
                send_sem=local_send.at[k], recv_sem=local_recv.at[k],
                device_id=(me, sibling), device_id_type=MESH,
            ).start()

    def local_wait(k):
        remote(
            local0.at[pl.ds(k * part, part)], local_send.at[k], local_recv.at[k], (me, sibling)
        ).wait_recv()

    def reach_wait():
        remote(reach0, reach_send, reach_recv, (me, sibling)).wait_recv()

    def pass_on(j, sends=True, receives=True):
        rs = pl.ds(pl.multiple_of(j * piece, piece), piece)
        if receives:
            remote(ent.at[j], chain_send.at[j], chain_recv.at[j], (me, sibling)).wait_recv()
            remote(ent.at[j], fwd_send.at[j], chain_recv.at[j], (me, sibling)).start()
            between = reach0[rs, :] * ent[j].astype(jnp.float32) + local0[rs, :]
        else:
            between = local0[rs, :]
        enter[rs, :] = between
        if sends:
            leave[j] = (reach[rs, :] * between + local[rs, :]).astype(jnp.bfloat16)
            pltpu.make_async_remote_copy(
                src_ref=leave.at[j], dst_ref=ent.at[j],
                send_sem=chain_send.at[j], recv_sem=chain_recv.at[j],
                device_id=(me, next_chip), device_id_type=MESH,
            ).start()

    def pass_chunk(k, sends, receives):
        if k == 0:
            reach_wait()
        local_wait(k)
        for j in range(k * per_chunk, (k + 1) * per_chunk):
            pass_on(j, sends, receives)

    def pass_all():
        reach_wait()
        for k in range(CHUNKS):
            local_wait(k)

        def step(j, carry):
            pass_on(j)
            return carry

        lax.fori_loop(0, PIECES, step, 0)

    def outputs(k):
        rs = slice(k * part, (k + 1) * part)
        for i in range(tiles):
            cols = slice(i * tile, (i + 1) * tile)
            s = enter[rs, cols]
            for t in range(frames):
                s = dec[t, rs, cols] * s + drv[t, rs, cols]
                states[t, :, cols] = s.astype(jnp.bfloat16)
        left_side = states[...].reshape(frames * part, width)
        square = None
        for i in range(tiles):
            cols = slice(i * tile, (i + 1) * tile)
            x = x_ref[:, rs, cols].reshape(frames * part, tile).astype(jnp.float32)
            m = x + nt(left_side, weight_rows(1, i))
            mixed[:, cols] = m
            square = m * m if i == 0 else square + m * m
        scaling = lax.rsqrt(jnp.sum(square, axis=1, keepdims=True) * (1.0 / width) + 1e-06)
        values = None
        for t in range(frames):
            ts = slice(t * part, (t + 1) * part)
            normed = (mixed[ts, :] * scaling[ts, :] * gain_ref[...]).astype(jnp.bfloat16)
            term = nt(normed, wb[t])
            values = term if t == 0 else values + term
        logits[rs, :] = values.astype(jnp.bfloat16)
        lane = lax.broadcasted_iota(jnp.int32, (part, LANES), 1)
        frame = (lane // bits).astype(jnp.float32)
        weight = jnp.where((len_b[rs, :] > frame) & (lane < packed), 1.0, 0.0)
        scaled = 4.0 * values
        size = jnp.abs(scaled)
        e = jnp.exp(-size)
        inverse = 1.0 / (1.0 + e)
        chance = jnp.where(scaled >= 0.0, inverse, e * inverse)
        entropy = jnp.log(1.0 + e) + size * e * inverse
        commit = jnp.square(jnp.abs(values) - 1.0)
        for row, value in enumerate((chance, entropy, commit, None)):
            kept = weight if value is None else value * weight
            sums[row:row + 1, :] += jnp.sum(kept, axis=0, keepdims=True)

    is_core1 = core == 1
    sibling_arrived(0)
    for k in range(CHUNKS):
        drives(k)
        if k >= 1:
            @pl.when(is_core1 & (chip == 0))
            def _():
                pass_chunk(k - 1, True, False)

    @pl.when(is_core1 & (chip == 0))
    def _():
        pass_chunk(CHUNKS - 1, True, False)

    @pl.when(is_core1 & (chip == 1) & (chip < chips - 1))
    def _():
        pass_all()

    for position in range(1, positions):
        p2_arrive(1, position)

    @pl.when(is_core1 & (chip > 1) & (chip < chips - 1))
    def _():
        pass_all()

    sibling_arrived(1)
    for k in range(CHUNKS):
        @pl.when(is_core1 & (chip == chips - 1))
        def _():
            pass_chunk(k, False, True)

        @pl.when(core == 0)
        def _():
            for j in range(k * per_chunk, (k + 1) * per_chunk):
                @pl.when(chip > 0)
                def _():
                    remote(ent.at[j], fwd_send.at[j], chain_recv.at[j], (me, sibling)).wait_recv()

                enter[j * piece:(j + 1) * piece, :] = ent[j].astype(jnp.float32)

        outputs(k)

    folded = sums[...]
    folded = folded + pltpu.roll(folded, LANES - 3 * bits, axis=1)
    folded = (
        folded + pltpu.roll(folded, LANES - bits, axis=1)
        + pltpu.roll(folded, LANES - 2 * bits, axis=1)
    )
    riding = pltpu.roll(folded, packed, axis=1)
    lane8 = lax.broadcasted_iota(jnp.int32, (8, LANES), 1)
    riding = jnp.where((lane8 >= packed) & (lane8 < packed + bits), riding, 0.0)
    dealt = nn(onehot[...], logits[...])
    sendbuf[...] = dealt.reshape(dp_count, 8, LANES) + riding[None]
    recvbuf[me, 0:GROUP] = sendbuf[me, 0:GROUP]

    def deal(step, carry):
        peer = (me + step) % dp_count
        pltpu.make_async_remote_copy(
            src_ref=sendbuf.at[peer, pl.ds(0, GROUP)], dst_ref=recvbuf.at[me, pl.ds(0, GROUP)],
            send_sem=a2a_send, recv_sem=a2a_recv, device_id=(peer, tm), device_id_type=MESH,
        ).start()
        return carry

    lax.fori_loop(1, dp_count, deal, 0)
    arrived = remote(
        recvbuf.at[pl.ds(0, dp_count - 1), pl.ds(0, GROUP)], a2a_send, a2a_recv, (me, sibling)
    )
    arrived.wait_recv()

    tmbuf[tm] = jnp.sum(recvbuf[...], axis=0)
    for step in range(1, tm_count):
        remote(tmbuf.at[tm], tm_send, tm_recv, (me, (tm + step) % tm_count)).start()

    turned = recvbuf[...].reshape(dp_count * 8, LANES).T.astype(jnp.bfloat16)
    placed = nn(turned, pick[...])
    for t in range(frames):
        codes_ref[t] = placed[t * bits:(t + 1) * bits, :].astype(jnp.bfloat16)

    tm_all = remote(tmbuf.at[pl.ds(0, tm_count - 1)], tm_send, tm_recv, (me, sibling))
    tm_all.wait_recv()
    totals = tmbuf[0]
    for i in range(1, tm_count):
        totals = totals + tmbuf[i]
    lane1 = lax.broadcasted_iota(jnp.int32, (1, LANES), 1)
    is_bit = (lane1 >= packed) & (lane1 < packed + bits)
    marginal = jnp.where(is_bit, totals[0:1] / totals[3:4], 0.5)
    terms = -marginal * jnp.log(marginal) - (1.0 - marginal) * jnp.log(1.0 - marginal)
    slots = 1.0 / float(rows * dp_count * frames * tm_count)
    shares = (totals[1:2] + 0.25 * totals[2:3]) * slots - terms
    penalty_ref[0, 0] = jnp.sum(jnp.where(is_bit, shares, 0.0))

    def sent(c):
        for w in range(2):
            p1_all(w, c).wait_send()
            for i in range(len(offsets)):
                remote(
                    group(w, c, major), p2_send.at[w], p2_recv.at[w, i], (me, sibling)
                ).wait_send()

    on_core(sent)
    remote(wt.at[0, mine], xs_send, xs_recv.at[0], (me, sibling)).wait_send()
    for w in range(2):
        ours = wt.at[w, pl.ds(2 * core, 2)]
        remote(ours, sib_send.at[w], sib_recv.at[w], (me, sibling)).wait_send()

    @pl.when(core == 0)
    def _():
        remote(reach, reach_send, reach_recv, (me, sibling)).wait_send()
        for k in range(CHUNKS):
            remote(
                local.at[pl.ds(k * part, part)], local_send.at[k], local_recv.at[k], (me, sibling)
            ).wait_send()

    @pl.when(is_core1)
    def _():
        for j in range(PIECES):
            @pl.when(chip < chips - 1)
            def _():
                remote(leave.at[j], chain_send.at[j], chain_recv.at[j], (me, sibling)).wait_send()

            @pl.when(chip > 0)
            def _():
                remote(ent.at[j], fwd_send.at[j], chain_recv.at[j], (me, sibling)).wait_send()

    arrived.wait_send()
    tm_all.wait_send()


def shards(latents, lengths, plan, w_in, w_down, w_up, w_out, rate, gain, w_bits):
    rows, frames, width = latents.shape
    dp_count, tm_count = lax.axis_size("dp"), lax.axis_size("tm")
    n = math.isqrt(dp_count)
    bits = w_bits.shape[1]
    narrow_width = w_down.shape[1]
    part = rows // CHUNKS
    block = width // dp_count
    vmem = pl.BlockSpec(memory_space=pltpu.VMEM)
    bf16, f32 = jnp.bfloat16, jnp.float32
    dma = pltpu.SemaphoreType.DMA
    codes, penalty = pl.pallas_call(
        functools.partial(kernel, dp_count, tm_count),
        out_shape=(
            jax.ShapeDtypeStruct((frames, bits, rows), bf16),
            jax.ShapeDtypeStruct((1, 1), f32),
        ),
        in_specs=[pl.BlockSpec(memory_space=pl.ANY)] + [vmem] * 9,
        out_specs=(vmem, pl.BlockSpec(memory_space=pltpu.SMEM)),
        scratch_shapes=[
            pltpu.VMEM((frames, rows, width), bf16),
            pltpu.VMEM((2, 4, n, n, block, width // 4), bf16),
            pltpu.VMEM((frames, rows, narrow_width), bf16),
            pltpu.VMEM((frames, rows, width), f32),
            pltpu.VMEM((frames, rows, width), f32),
            pltpu.VMEM((rows, width), f32),
            pltpu.VMEM((rows, width), f32),
            pltpu.VMEM((rows, width), f32),
            pltpu.VMEM((rows, width), f32),
            pltpu.VMEM((PIECES, rows // PIECES, width), bf16),
            pltpu.VMEM((PIECES, rows // PIECES, width), bf16),
            pltpu.VMEM((rows, width), f32),
            pltpu.VMEM((frames, part, width), bf16),
            pltpu.VMEM((frames * part, width), f32),
            pltpu.VMEM((frames, LANES, width), bf16),
            pltpu.VMEM((dp_count * 8, rows), bf16),
            pltpu.VMEM((dp_count * 8, rows), bf16),
            pltpu.VMEM((rows, LANES), f32),
            pltpu.VMEM((rows, LANES), bf16),
            pltpu.VMEM((8, LANES), f32),
            pltpu.VMEM((dp_count, 8, LANES), f32),
            pltpu.VMEM((dp_count, 8, LANES), f32),
            pltpu.VMEM((tm_count, 8, LANES), f32),
            dma,
            dma((2,)), dma((2,)), dma((2,)), dma((2, n - 1)),
            dma, dma((n,)), dma((2,)), dma((2,)),
            dma, dma, dma((CHUNKS,)), dma((CHUNKS,)),
            dma((PIECES,)), dma((PIECES,)), dma((PIECES,)),
            dma, dma, dma, dma,
        ],
        compiler_params=pltpu.CompilerParams(
            collective_id=0, has_side_effects=True, vmem_limit_bytes=56 * 1024 * 1024
        ),
    )(
        jnp.transpose(latents, (1, 0, 2)), lengths.reshape(1, rows), plan.reshape(1, rows),
        w_in.T, w_down.T, w_up, w_out.T, rate.reshape(1, width), gain.reshape(1, width), w_bits.T,
    )
    return jnp.transpose(codes, (1, 0, 2)), penalty[0, 0]


def solution(mesh):
    return jax.shard_map(
        shards,
        mesh=mesh,
        in_specs=(
            P("dp", "tm", None),
            P("dp"),
            P("dp"),
            P(None, "dp"),
            P(),
            P(),
            P(None, "dp"),
            P(),
            P(),
            P(),
        ),
        out_specs=(P(None, "tm", "dp"), P()),
        check_vma=False,
    )
```

time: 87.8 us -> 76.3 us (0.87)
  Pallas kernels: 83.7 us -> 72.2 us
    pallas_call x1, Pallas kernels: 83.7 us -> 72.2 us  [shards(): pl.pallas_call(functools.partial(kernel, dp_count, tm_count), out_shape=(...]
where the time goes in v2:
time: 76.3 us; the launch traced here: 76.1 us
  Pallas kernels  72.2 us (95%)
  between operations  2.33 us (3%)
  local copies, waits for them, and re-layouts  1.53 us (2%)
    pallas_call x1, Pallas kernels, shards(): pl.pallas_call(functools.partial(kernel, dp_count, tm_count), out_shape=(...  72.2 us
    unnamed x1, local copies, waits for them, and re-layouts  1.53 us

profile of v2, /device:TPU:1, one launch (start us, length us, event | category | flops | bytes accessed | tf_op | source)
XLA Modules:
  0.0 76.1 jit_solution(16961198524286878024)
XLA Ops:
  0.6 72.2 %shard_map.113 = (bf16[6,18,256]{2,1,0:T(8,128)(2,1)}, f32[1,1]{1,0:T(1,128)}) custom-call(bf16[6,256,1024]{2,1,0:T(8,128)(2,1)} %bitcast.11, s32[1,256]{1,0:T(1,128)} %bitcast.19, s32[1,256]{1,0:T(1,128)} %bitcast.20, bf16[16,1024]{1,0:T(8,128)(2,1)} %bitcast.15, bf16[64,1024]{1,0:T(8,128)(2,1)} %bitcast.12, bf16[64,1024]{1,0:T(8,128)(2,1)} %wup_ref.1, ...), custom_call_target="tpu_custom_call" | custom-call | tf_op jit(solution)/shard_map/pallas_call | solution.py:489
  72.9 1.5 %copy.12 = bf16[18,6,256]{2,1,0:T(8,128)(2,1)} copy(bf16[18,6,256]{2,0,1:T(8,128)(2,1)} %bitcast.13) | data formatting | bytes 110592

commit v3 on v2

--- a/solution.py
+++ b/solution.py
@@ -25,14 +25,19 @@
 
 
 def kernel(
-    dp_count, tm_count, x_hbm, lengths_ref, plan_ref, win_ref, wdown_ref, wup_ref, wout_ref, rate_ref,
-    gain_ref, wbits_ref, codes_ref, penalty_ref,
-    x_ref, wt, narrow, dec, drv, reach, local, reach0, local0, ent, leave, enter, states, mixed, wb,
-    onehot, pick, len_b, logits, sums, sendbuf, recvbuf, tmbuf,
-    x_sem, p1_send, p1_recv, p2_send, p2_recv, xs_send, xs_recv, sib_send, sib_recv,
-    reach_send, reach_recv, local_send, local_recv, chain_send, chain_recv, fwd_send,
-    a2a_send, a2a_recv, tm_send, tm_recv,
+    dp_count, tm_count, x_hbm, *refs,
 ):
+    smalls, refs = refs[:9], refs[9:]
+    codes_ref, penalty_ref, *refs = refs
+    lengths_ref, plan_ref, win_ref, wdown_ref, wup_ref, wout_ref, rate_ref, gain_ref, wbits_ref = refs[:9]
+    small_sem, *refs = refs[9:]
+    (
+        x_ref, wt, narrow, dec, drv, reach, local, reach0, local0, ent, leave, enter, states, mixed, wb,
+        onehot, pick, len_b, logits, sums, sendbuf, recvbuf, tmbuf,
+        x_sem, p1_send, p1_recv, p2_send, p2_recv, xs_send, xs_recv, sib_send, sib_recv,
+        reach_send, reach_recv, local_send, local_recv, chain_send, chain_recv, fwd_send,
+        a2a_send, a2a_recv, tm_send, tm_recv,
+    ) = refs
     frames, rows, width = x_ref.shape
     n = math.isqrt(dp_count)
     quarter = width // 4
@@ -64,12 +69,16 @@
         pl.when(core == 0)(lambda: make(0))
         pl.when(core == 1)(lambda: make(1))
 
-    offsets = [o for step in range(1, n // 2) for o in (step, -step)] + [n // 2]
+    near = n // 4
+    items = [(0, 0, n)]
+    if n == 2:
+        items += [(1, 0, n)]
+    else:
+        items += [(o, 0, n) for step in range(1, n // 2) for o in (-step, step)]
+        items += [(n // 2, 0, n // 2), (n // 2, n // 2, n // 2)]
+    early = 2 * near if n > 2 else 1
 
     x_copy = pltpu.make_async_copy(x_hbm, x_ref, x_sem)
-    x_copy.start()
-    recvbuf[...] = jnp.zeros_like(recvbuf)
-
     barrier = pltpu.get_barrier_semaphore()
 
     def greet(dp_id, tm_id):
@@ -82,6 +91,18 @@
     for step in range(1, tm_count):
         greet(me, (tm + step) % tm_count)
 
+    small_copies = [
+        pltpu.make_async_copy(source, target, small_sem.at[i])
+        for i, (source, target) in enumerate(zip(smalls, (
+            lengths_ref, plan_ref, win_ref, wdown_ref, wup_ref, wout_ref, rate_ref, gain_ref, wbits_ref
+        )))
+    ]
+    for i in (2, 5, 3, 4, 6, 0, 1, 7, 8):
+        small_copies[i].start()
+    x_copy.start()
+    small_copies[2].wait()
+    small_copies[5].wait()
+
     wt[0, mine, y, z] = win_ref[:, pl.ds(pl.multiple_of(mine * quarter, quarter), quarter)]
     for i in range(2):
         start = pl.multiple_of((2 * core + i) * quarter, quarter)
@@ -91,6 +112,7 @@
     def _():
         ent[...] = jnp.zeros_like(ent)
 
+    recvbuf[...] = jnp.zeros_like(recvbuf)
     pl.semaphore_wait(barrier, 2 * (n - 1) + (tm_count - 1))
 
     def remote(ref, send, recv, device):
@@ -107,53 +129,77 @@
             return wt.at[w, quarters, major_id, pl.ds(low, count)]
         return wt.at[w, quarters, pl.ds(low, count), major_id]
 
-    def group_id(position):
-        return major if position == 0 else (major + 2 * n - offsets[position - 1]) % n
+    def at(offset):
+        return (major + n + offset) % n
+
+    def held(w, c, item, first=None):
+        offset, low, count = items[item]
+        return group(w, c, at(offset), first, low, count)
+
+    def quarters_of(w):
+        return pl.ds(firsts[w], counts[w])
 
     def p1_start(w):
         for step in range(1, n):
             remote(
-                wt.at[w, pl.ds(firsts[w], counts[w]), y, z], p1_send.at[w], p1_recv.at[w],
+                wt.at[w, quarters_of(w), y, z], p1_send.at[w], p1_recv.at[w],
                 (dp_of(major, (minor + step) % n), tm),
             ).start()
 
-    def p1_all(w, c):
-        return remote(
-            group(w, c, major, None, 0, n - 1), p1_send.at[w], p1_recv.at[w], (me, sibling)
-        )
-
-    def p2_start(w):
+    def p1_all(w):
+        some = wt.at[w, quarters_of(w), 0, pl.ds(0, n - 1)]
+        return remote(some, p1_send.at[w], p1_recv.at[w], (me, sibling))
+
+    def p2_all(w):
+        some = wt.at[w, quarters_of(w), pl.ds(0, n - 1)]
+        return remote(some, p2_send.at[w], p2_recv.at[w, 0], (me, sibling))
+
+    def send_group(w, piece_ref, item, toward):
+        remote(
+            piece_ref, p2_send.at[w], p2_recv.at[w, item - 1], (dp_of(at(toward), minor), tm)
+        ).start()
+
+    def near_sends(w):
+        p1_all(w).wait_recv()
+
         def make(c):
-            p1_all(w, c).wait_recv()
-            for i, offset in enumerate(offsets):
-                remote(
-                    group(w, c, major), p2_send.at[w], p2_recv.at[w, i],
-                    (dp_of((major + offset + n) % n, minor), tm),
-                ).start()
+            for item in range(1, early + 1):
+                send_group(w, group(w, c, major), item, -items[item][0])
             forward(w, c, 0)
         on_core(make)
 
-    def forward(w, c, position):
-        held = group(w, c, group_id(position))
+    def far_sends(w, c, item):
+        offset = items[item][0]
+        if n == 2 or item > early:
+            return
+        side = 1 if offset > 0 else -1
+        if abs(offset) + near < n // 2:
+            send_group(w, held(w, c, item), items.index((offset + side * near, 0, n)), -side * near)
+        else:
+            low = 0 if side < 0 else n // 2
+            target = items.index((n // 2, low, n // 2))
+            send_group(w, group(w, c, at(offset), None, low, n // 2), target, -side * near)
+
+    def forward(w, c, item):
         if w == 0:
-            target = next_chip if position % 2 == 0 else last_chip
-            remote(held, xs_send, xs_recv.at[position], (me, target)).start()
-        remote(held, sib_send.at[w], sib_recv.at[w], (me, sibling)).start()
-
-    def p2_arrive(w, position):
+            target = next_chip if item % 2 == 0 and item < n - 1 else last_chip
+            remote(held(w, c, item), xs_send, xs_recv.at[item], (me, target)).start()
+        remote(held(w, c, item), sib_send.at[w], sib_recv.at[w], (me, sibling)).start()
+
+    def arrive(w, item):
         def make(c):
             remote(
-                group(w, c, group_id(position)), p2_send.at[w], p2_recv.at[w, position - 1],
-                (me, sibling),
+                held(w, c, item), p2_send.at[w], p2_recv.at[w, item - 1], (me, sibling)
             ).wait_recv()
-            forward(w, c, position)
+            far_sends(w, c, item)
+            forward(w, c, item)
         on_core(make)
 
-    def x_arrive(position):
+    def x_arrive(item):
         def make(c):
-            held = group(0, c, group_id(position), other)
-            remote(held, xs_send, xs_recv.at[position], (me, sibling)).wait_recv()
-            remote(held, sib_send.at[0], sib_recv.at[0], (me, sibling)).start()
+            theirs = held(0, c, item, other)
+            remote(theirs, xs_send, xs_recv.at[item], (me, sibling)).wait_recv()
+            remote(theirs, sib_send.at[0], sib_recv.at[0], (me, sibling)).start()
         on_core(make)
 
     def sibling_arrived(w):
@@ -161,6 +207,8 @@
         remote(theirs, sib_send.at[w], sib_recv.at[w], (me, sibling)).wait_recv()
 
     def small_things():
+        for i in (0, 1, 7, 8):
+            small_copies[i].wait()
         first = tm * frames
         lengths = jnp.broadcast_to(lengths_ref[...].astype(jnp.float32), (LANES, rows))
         len_b[...] = lengths.T - first.astype(jnp.float32)
@@ -183,6 +231,8 @@
         sums[...] = jnp.zeros_like(sums)
 
     def narrowing():
+        for i in (3, 4, 6):
+            small_copies[i].wait()
         x_copy.wait()
         for t in range(frames):
             narrow[t] = nt(x_ref[t], wdown_ref[...]).astype(jnp.bfloat16)
@@ -200,29 +250,23 @@
         for t in range(low, min(high, frames)):
             decays(t)
 
-    positions = len(offsets) + 1
+    count = len(items)
     p1_start(0)
     narrowing()
     decay_frames(0, 1)
-    p2_start(0)
+    near_sends(0)
+    p1_start(1)
     decay_frames(1, 3)
+    for item in range(1, early + 1):
+        arrive(0, item)
+    near_sends(1)
+    decay_frames(3, 4)
     x_done = 0
-    for position in range(1, positions):
-        p2_arrive(0, position)
-        if position == 1:
-            p1_start(1)
-        if position == positions - 2 or positions == 2:
-            p2_start(1)
-        if position >= 4:
-            x_arrive(x_done)
-            x_done += 1
-        if position == min(4, positions - 1):
-            decay_frames(3, 4)
-    decay_frames(4, 5)
-    while x_done < positions - 2:
+    for item in range(early + 1, count):
         x_arrive(x_done)
         x_done += 1
-    decay_frames(5, frames)
+        arrive(0, item)
+    decay_frames(4, frames)
 
     @pl.when(core == 0)
     def _():
@@ -232,7 +276,7 @@
         ).start()
 
     small_things()
-    while x_done < positions:
+    while x_done < count:
         x_arrive(x_done)
         x_done += 1
 
@@ -356,6 +400,9 @@
             @pl.when(is_core1 & (chip == 0))
             def _():
                 pass_chunk(k - 1, True, False)
+        if k == 0:
+            for item in range(1, early + 1):
+                arrive(1, item)
 
     @pl.when(is_core1 & (chip == 0))
     def _():
@@ -365,8 +412,8 @@
     def _():
         pass_all()
 
-    for position in range(1, positions):
-        p2_arrive(1, position)
+    for item in range(early + 1, count):
+        arrive(1, item)
 
     @pl.when(is_core1 & (chip > 1) & (chip < chips - 1))
     def _():
@@ -402,15 +449,51 @@
     sendbuf[...] = dealt.reshape(dp_count, 8, LANES) + riding[None]
     recvbuf[me, 0:GROUP] = sendbuf[me, 0:GROUP]
 
-    def deal(step, carry):
-        peer = (me + step) % dp_count
+    def from_far(i):
+        return n // 2 + (i // 2) * (1 - 2 * (i % 2)) - i % 2
+
+    def deal(step):
+        peer = (y + from_far(step // n)) % n * n + (z + from_far(step % n)) % n
         pltpu.make_async_remote_copy(
             src_ref=sendbuf.at[peer, pl.ds(0, GROUP)], dst_ref=recvbuf.at[me, pl.ds(0, GROUP)],
             send_sem=a2a_send, recv_sem=a2a_recv, device_id=(peer, tm), device_id_type=MESH,
         ).start()
+
+    unrolled = 3 if (dp_count - 1) % 3 == 0 else 1
+
+    def deal_some(i, carry):
+        for j in range(unrolled):
+            deal(i * unrolled + j)
         return carry
 
-    lax.fori_loop(1, dp_count, deal, 0)
+    lax.fori_loop(0, (dp_count - 1) // unrolled, deal_some, 0)
+
+    for w in range(2):
+        p1_all(w).wait_send()
+        p2_all(w).wait_send()
+        ours = wt.at[w, pl.ds(2 * core, 2)]
+        remote(ours, sib_send.at[w], sib_recv.at[w], (me, sibling)).wait_send()
+    remote(wt.at[0, mine], xs_send, xs_recv.at[0], (me, sibling)).wait_send()
+
+    @pl.when(core == 0)
+    def _():
+        remote(reach, reach_send, reach_recv, (me, sibling)).wait_send()
+        for k in range(CHUNKS):
+            remote(
+                local.at[pl.ds(k * part, part)], local_send.at[k], local_recv.at[k], (me, sibling)
+            ).wait_send()
+
+    @pl.when(is_core1)
+    def _():
+        for j in range(PIECES):
+            @pl.when(chip < chips - 1)
+            def _():
+                remote(leave.at[j], chain_send.at[j], chain_recv.at[j], (me, sibling)).wait_send()
+
+            @pl.when(chip > 0)
+            def _():
+                remote(ent.at[j], fwd_send.at[j], chain_recv.at[j], (me, sibling)).wait_send()
+
     arrived = remote(
         recvbuf.at[pl.ds(0, dp_count - 1), pl.ds(0, GROUP)], a2a_send, a2a_recv, (me, sibling)
     )
@@ -437,39 +520,6 @@
     slots = 1.0 / float(rows * dp_count * frames * tm_count)
     shares = (totals[1:2] + 0.25 * totals[2:3]) * slots - terms
     penalty_ref[0, 0] = jnp.sum(jnp.where(is_bit, shares, 0.0))
-
-    def sent(c):
-        for w in range(2):
-            p1_all(w, c).wait_send()
-            for i in range(len(offsets)):
-                remote(
-                    group(w, c, major), p2_send.at[w], p2_recv.at[w, i], (me, sibling)
-                ).wait_send()
-
-    on_core(sent)
-    remote(wt.at[0, mine], xs_send, xs_recv.at[0], (me, sibling)).wait_send()
-    for w in range(2):
-        ours = wt.at[w, pl.ds(2 * core, 2)]
-        remote(ours, sib_send.at[w], sib_recv.at[w], (me, sibling)).wait_send()
-
-    @pl.when(core == 0)
-    def _():
-        remote(reach, reach_send, reach_recv, (me, sibling)).wait_send()
-        for k in range(CHUNKS):
-            remote(
-                local.at[pl.ds(k * part, part)], local_send.at[k], local_recv.at[k], (me, sibling)
-            ).wait_send()
-
-    @pl.when(is_core1)
-    def _():
-        for j in range(PIECES):
-            @pl.when(chip < chips - 1)
-            def _():
-                remote(leave.at[j], chain_send.at[j], chain_recv.at[j], (me, sibling)).wait_send()
-
-            @pl.when(chip > 0)
-            def _():
-                remote(ent.at[j], fwd_send.at[j], chain_recv.at[j], (me, sibling)).wait_send()
 
     arrived.wait_send()
     tm_all.wait_send()
@@ -492,9 +542,19 @@
             jax.ShapeDtypeStruct((frames, bits, rows), bf16),
             jax.ShapeDtypeStruct((1, 1), f32),
         ),
-        in_specs=[pl.BlockSpec(memory_space=pl.ANY)] + [vmem] * 9,
+        in_specs=[pl.BlockSpec(memory_space=pl.ANY)] * 10,
         out_specs=(vmem, pl.BlockSpec(memory_space=pltpu.SMEM)),
         scratch_shapes=[
+            pltpu.VMEM((1, rows), jnp.int32),
+            pltpu.VMEM((1, rows), jnp.int32),
+            pltpu.VMEM((block, width), bf16),
+            pltpu.VMEM((narrow_width, width), bf16),
+            pltpu.VMEM((narrow_width, width), bf16),
+            pltpu.VMEM((block, width), bf16),
+            pltpu.VMEM((1, width), f32),
+            pltpu.VMEM((1, width), f32),
+            pltpu.VMEM((bits, width), bf16),
+            dma((9,)),
             pltpu.VMEM((frames, rows, width), bf16),
             pltpu.VMEM((2, 4, n, n, block, width // 4), bf16),
             pltpu.VMEM((frames, rows, narrow_width), bf16),
@@ -519,8 +579,8 @@
             pltpu.VMEM((dp_count, 8, LANES), f32),
             pltpu.VMEM((tm_count, 8, LANES), f32),
             dma,
-            dma((2,)), dma((2,)), dma((2,)), dma((2, n - 1)),
-            dma, dma((n,)), dma((2,)), dma((2,)),
+            dma((2,)), dma((2,)), dma((2,)), dma((2, n)),
+            dma, dma((n + 1,)), dma((2,)), dma((2,)),
             dma, dma, dma((CHUNKS,)), dma((CHUNKS,)),
             dma((PIECES,)), dma((PIECES,)), dma((PIECES,)),
             dma, dma, dma, dma,

time: 76.3 us -> 72.3 us (0.948)
  Pallas kernels: 72.2 us -> 68.3 us
    pallas_call x1, Pallas kernels: 72.2 us -> 68.3 us  [shards(): pl.pallas_call(functools.partial(kernel, dp_count, tm_count), out_shape=(...]
where the time goes in v3:
time: 72.3 us; the launch traced here: 72.2 us
  Pallas kernels  68.3 us (94%)
  between operations  2.33 us (3%)
  local copies, waits for them, and re-layouts  1.53 us (2%)
    pallas_call x1, Pallas kernels, shards(): pl.pallas_call(functools.partial(kernel, dp_count, tm_count), out_shape=(...  68.3 us
    unnamed x1, local copies, waits for them, and re-layouts  1.53 us

profile of v3, /device:TPU:1, one launch (start us, length us, event | category | flops | bytes accessed | tf_op | source)
XLA Modules:
  0.0 72.2 jit_solution(6807542868918504898)
XLA Ops:
  0.6 68.3 %shard_map.113 = (bf16[6,18,256]{2,1,0:T(8,128)(2,1)}, f32[1,1]{1,0:T(1,128)}) custom-call(bf16[6,256,1024]{2,1,0:T(8,128)(2,1)} %bitcast.11, s32[1,256]{1,0:T(1,128)} %bitcast.19, s32[1,256]{1,0:T(1,128)} %bitcast.20, bf16[16,1024]{1,0:T(8,128)(2,1)} %bitcast.15, bf16[64,1024]{1,0:T(8,128)(2,1)} %bitcast.12, bf16[64,1024]{1,0:T(8,128)(2,1)} %refs_4_.1, ...), custom_call_target="tpu_custom_call" | custom-call | tf_op jit(solution)/shard_map/pallas_call | solution.py:539
  68.9 1.5 %copy.12 = bf16[18,6,256]{2,1,0:T(8,128)(2,1)} copy(bf16[18,6,256]{2,0,1:T(8,128)(2,1)} %bitcast.13) | data formatting | bytes 110592

commit v4 on v3

--- a/solution.py
+++ b/solution.py
@@ -12,7 +12,7 @@
 GROUP = 4
 LANES = 128
 CHUNKS = 4
-PIECES = 8
+PIECES = 16
 LOG2E = math.log2(math.e)
 
 
@@ -33,10 +33,10 @@
     small_sem, *refs = refs[9:]
     (
         x_ref, wt, narrow, dec, drv, reach, local, reach0, local0, ent, leave, enter, states, mixed, wb,
-        onehot, pick, len_b, logits, sums, sendbuf, recvbuf, tmbuf,
+        onehot, pick, len_b, logits, sums, sendbuf, recvbuf, tmbuf, zbuf, ybuf, staged,
         x_sem, p1_send, p1_recv, p2_send, p2_recv, xs_send, xs_recv, sib_send, sib_recv,
         reach_send, reach_recv, local_send, local_recv, chain_send, chain_recv, fwd_send,
-        a2a_send, a2a_recv, tm_send, tm_recv,
+        a2a_send, a2a_recv, sum_send, sum_recv, store_sem,
     ) = refs
     frames, rows, width = x_ref.shape
     n = math.isqrt(dp_count)
@@ -225,9 +225,8 @@
         onehot[...] = chosen.T.astype(jnp.bfloat16)
         place = lax.broadcasted_iota(jnp.int32, (LANES, bits), 0)
         bit = lax.broadcasted_iota(jnp.int32, (LANES, bits), 1)
-        for t in range(frames):
-            chooser = jnp.where(place == bit + t * bits, 1.0, 0.0).astype(jnp.bfloat16)
-            wb[t] = nn(chooser, wbits_ref[...]).astype(jnp.bfloat16)
+        chooser = jnp.where(place == bit, 1.0, 0.0).astype(jnp.bfloat16)
+        wb[...] = nn(chooser, wbits_ref[...]).astype(jnp.bfloat16)
         sums[...] = jnp.zeros_like(sums)
 
     def narrowing():
@@ -343,16 +342,17 @@
         for j in range(k * per_chunk, (k + 1) * per_chunk):
             pass_on(j, sends, receives)
 
-    def pass_all():
-        reach_wait()
-        for k in range(CHUNKS):
+    def pass_half(h):
+        if h == 0:
+            reach_wait()
+        for k in range(h * CHUNKS // 2, (h + 1) * CHUNKS // 2):
             local_wait(k)
 
         def step(j, carry):
             pass_on(j)
             return carry
 
-        lax.fori_loop(0, PIECES, step, 0)
+        lax.fori_loop(h * PIECES // 2, (h + 1) * PIECES // 2, step, 0)
 
     def outputs(k):
         rs = slice(k * part, (k + 1) * part)
@@ -371,12 +371,11 @@
             mixed[:, cols] = m
             square = m * m if i == 0 else square + m * m
         scaling = lax.rsqrt(jnp.sum(square, axis=1, keepdims=True) * (1.0 / width) + 1e-06)
-        values = None
-        for t in range(frames):
-            ts = slice(t * part, (t + 1) * part)
-            normed = (mixed[ts, :] * scaling[ts, :] * gain_ref[...]).astype(jnp.bfloat16)
-            term = nt(normed, wb[t])
-            values = term if t == 0 else values + term
+        normed = (mixed[...] * scaling * gain_ref[...]).astype(jnp.bfloat16)
+        by_frame = nt(normed, wb[...])
+        values = by_frame[0:part]
+        for t in range(1, frames):
+            values = values + pltpu.roll(by_frame[t * part:(t + 1) * part], t * bits, axis=1)
         logits[rs, :] = values.astype(jnp.bfloat16)
         lane = lax.broadcasted_iota(jnp.int32, (part, LANES), 1)
         frame = (lane // bits).astype(jnp.float32)
@@ -410,14 +409,19 @@
 
     @pl.when(is_core1 & (chip == 1) & (chip < chips - 1))
     def _():
-        pass_all()
+        pass_half(0)
+        pass_half(1)
+
+    @pl.when(is_core1 & (chip > 1) & (chip < chips - 1))
+    def _():
+        pass_half(0)
 
     for item in range(early + 1, count):
         arrive(1, item)
 
     @pl.when(is_core1 & (chip > 1) & (chip < chips - 1))
     def _():
-        pass_all()
+        pass_half(1)
 
     sibling_arrived(1)
     for k in range(CHUNKS):
@@ -436,17 +440,29 @@
 
         outputs(k)
 
-    folded = sums[...]
-    folded = folded + pltpu.roll(folded, LANES - 3 * bits, axis=1)
-    folded = (
-        folded + pltpu.roll(folded, LANES - bits, axis=1)
-        + pltpu.roll(folded, LANES - 2 * bits, axis=1)
-    )
-    riding = pltpu.roll(folded, packed, axis=1)
-    lane8 = lax.broadcasted_iota(jnp.int32, (8, LANES), 1)
-    riding = jnp.where((lane8 >= packed) & (lane8 < packed + bits), riding, 0.0)
+    def share(buffer, own, stage, value, peer_of):
+        buffer[own] = value
+        for step in range(1, buffer.shape[0]):
+            remote(
+                buffer.at[own], sum_send.at[stage], sum_recv.at[stage], peer_of(step)
+            ).start()
+
+    def shared(buffer, stage):
+        return remote(
+            buffer.at[pl.ds(0, buffer.shape[0] - 1)], sum_send.at[stage], sum_recv.at[stage],
+            (me, sibling),
+        )
+
+    def total_of(buffer, stage):
+        shared(buffer, stage).wait_recv()
+        total = buffer[0]
+        for i in range(1, buffer.shape[0]):
+            total = total + buffer[i]
+        return total
+
+    share(tmbuf, tm, 0, sums[...], lambda step: (me, (tm + step) % tm_count))
     dealt = nn(onehot[...], logits[...])
-    sendbuf[...] = dealt.reshape(dp_count, 8, LANES) + riding[None]
+    sendbuf[...] = dealt.reshape(dp_count, 8, LANES)
     recvbuf[me, 0:GROUP] = sendbuf[me, 0:GROUP]
 
     def from_far(i):
@@ -468,6 +484,8 @@
 
     lax.fori_loop(0, (dp_count - 1) // unrolled, deal_some, 0)
 
+    share(zbuf, z, 1, total_of(tmbuf, 0), lambda step: (y * n + (z + step) % n, tm))
+
     for w in range(2):
         p1_all(w).wait_send()
         p2_all(w).wait_send()
@@ -497,32 +515,32 @@
     arrived = remote(
         recvbuf.at[pl.ds(0, dp_count - 1), pl.ds(0, GROUP)], a2a_send, a2a_recv, (me, sibling)
     )
+    share(ybuf, y, 2, total_of(zbuf, 1), lambda step: ((y + step) % n * n + z, tm))
+    for stage, buffer in enumerate((tmbuf, zbuf)):
+        shared(buffer, stage).wait_send()
+    arrived.wait_send()
     arrived.wait_recv()
-
-    tmbuf[tm] = jnp.sum(recvbuf[...], axis=0)
-    for step in range(1, tm_count):
-        remote(tmbuf.at[tm], tm_send, tm_recv, (me, (tm + step) % tm_count)).start()
-
     turned = recvbuf[...].reshape(dp_count * 8, LANES).T.astype(jnp.bfloat16)
     placed = nn(turned, pick[...])
     for t in range(frames):
-        codes_ref[t] = placed[t * bits:(t + 1) * bits, :].astype(jnp.bfloat16)
-
-    tm_all = remote(tmbuf.at[pl.ds(0, tm_count - 1)], tm_send, tm_recv, (me, sibling))
-    tm_all.wait_recv()
-    totals = tmbuf[0]
-    for i in range(1, tm_count):
-        totals = totals + tmbuf[i]
-    lane1 = lax.broadcasted_iota(jnp.int32, (1, LANES), 1)
-    is_bit = (lane1 >= packed) & (lane1 < packed + bits)
-    marginal = jnp.where(is_bit, totals[0:1] / totals[3:4], 0.5)
+        staged[t] = placed[t * bits:(t + 1) * bits, :].astype(jnp.bfloat16)
+    store = pltpu.make_async_copy(staged, codes_ref, store_sem)
+    store.start()
+
+    folded = total_of(ybuf, 2)
+    folded = folded + pltpu.roll(folded, LANES - 3 * bits, axis=1)
+    folded = (
+        folded + pltpu.roll(folded, LANES - bits, axis=1)
+        + pltpu.roll(folded, LANES - 2 * bits, axis=1)
+    )
+    is_bit = lax.broadcasted_iota(jnp.int32, (1, LANES), 1) < bits
+    marginal = jnp.where(is_bit, folded[0:1] / folded[3:4], 0.5)
     terms = -marginal * jnp.log(marginal) - (1.0 - marginal) * jnp.log(1.0 - marginal)
     slots = 1.0 / float(rows * dp_count * frames * tm_count)
-    shares = (totals[1:2] + 0.25 * totals[2:3]) * slots - terms
+    shares = (folded[1:2] + 0.25 * folded[2:3]) * slots - terms
     penalty_ref[0, 0] = jnp.sum(jnp.where(is_bit, shares, 0.0))
-
-    arrived.wait_send()
-    tm_all.wait_send()
+    shared(ybuf, 2).wait_send()
+    store.wait()
 
 
 def shards(latents, lengths, plan, w_in, w_down, w_up, w_out, rate, gain, w_bits):
@@ -533,7 +551,6 @@
     narrow_width = w_down.shape[1]
     part = rows // CHUNKS
     block = width // dp_count
-    vmem = pl.BlockSpec(memory_space=pltpu.VMEM)
     bf16, f32 = jnp.bfloat16, jnp.float32
     dma = pltpu.SemaphoreType.DMA
     codes, penalty = pl.pallas_call(
@@ -543,7 +560,7 @@
             jax.ShapeDtypeStruct((1, 1), f32),
         ),
         in_specs=[pl.BlockSpec(memory_space=pl.ANY)] * 10,
-        out_specs=(vmem, pl.BlockSpec(memory_space=pltpu.SMEM)),
+        out_specs=(pl.BlockSpec(memory_space=pl.ANY), pl.BlockSpec(memory_space=pltpu.SMEM)),
         scratch_shapes=[
             pltpu.VMEM((1, rows), jnp.int32),
             pltpu.VMEM((1, rows), jnp.int32),
@@ -569,7 +586,7 @@
             pltpu.VMEM((rows, width), f32),
             pltpu.VMEM((frames, part, width), bf16),
             pltpu.VMEM((frames * part, width), f32),
-            pltpu.VMEM((frames, LANES, width), bf16),
+            pltpu.VMEM((LANES, width), bf16),
             pltpu.VMEM((dp_count * 8, rows), bf16),
             pltpu.VMEM((dp_count * 8, rows), bf16),
             pltpu.VMEM((rows, LANES), f32),
@@ -578,12 +595,15 @@
             pltpu.VMEM((dp_count, 8, LANES), f32),
             pltpu.VMEM((dp_count, 8, LANES), f32),
             pltpu.VMEM((tm_count, 8, LANES), f32),
+            pltpu.VMEM((n, 8, LANES), f32),
+            pltpu.VMEM((n, 8, LANES), f32),
+            pltpu.VMEM((frames, bits, rows), bf16),
             dma,
             dma((2,)), dma((2,)), dma((2,)), dma((2, n)),
             dma, dma((n + 1,)), dma((2,)), dma((2,)),
             dma, dma, dma((CHUNKS,)), dma((CHUNKS,)),
             dma((PIECES,)), dma((PIECES,)), dma((PIECES,)),
-            dma, dma, dma, dma,
+            dma, dma, dma((3,)), dma((3,)), dma,
         ],
         compiler_params=pltpu.CompilerParams(
             collective_id=0, has_side_effects=True, vmem_limit_bytes=56 * 1024 * 1024

time: 72.3 us -> 68.7 us (0.950)
  Pallas kernels: 68.3 us -> 64.7 us
    pallas_call x1, Pallas kernels: 68.3 us -> 64.7 us  [shards(): pl.pallas_call(functools.partial(kernel, dp_count, tm_count), out_shape=(...]
where the time goes in v4:
time: 68.7 us; the launch traced here: 68.6 us
  Pallas kernels  64.7 us (94%)
  between operations  2.33 us (3%)
  local copies, waits for them, and re-layouts  1.53 us (2%)
    pallas_call x1, Pallas kernels, shards(): pl.pallas_call(functools.partial(kernel, dp_count, tm_count), out_shape=(...  64.7 us
    unnamed x1, local copies, waits for them, and re-layouts  1.53 us

profile of v4, /device:TPU:1, one launch (start us, length us, event | category | flops | bytes accessed | tf_op | source)
XLA Modules:
  0.0 68.6 jit_solution(16530741974191143230)
XLA Ops:
  0.6 64.7 %shard_map.113 = (bf16[6,18,256]{2,1,0:T(8,128)(2,1)}, f32[1,1]{1,0:T(1,128)}) custom-call(bf16[6,256,1024]{2,1,0:T(8,128)(2,1)} %bitcast.11, s32[1,256]{1,0:T(1,128)} %bitcast.19, s32[1,256]{1,0:T(1,128)} %bitcast.20, bf16[16,1024]{1,0:T(8,128)(2,1)} %bitcast.15, bf16[64,1024]{1,0:T(8,128)(2,1)} %bitcast.12, bf16[64,1024]{1,0:T(8,128)(2,1)} %refs_4_.1, ...), custom_call_target="tpu_custom_call" | custom-call | tf_op jit(solution)/shard_map/pallas_call | solution.py:556
  65.3 1.5 %copy.12 = bf16[18,6,256]{2,1,0:T(8,128)(2,1)} copy(bf16[18,6,256]{2,0,1:T(8,128)(2,1)} %bitcast.13) | data formatting | bytes 110592

commit v5 on v4

--- a/solution.py
+++ b/solution.py
@@ -33,10 +33,10 @@
     small_sem, *refs = refs[9:]
     (
         x_ref, wt, narrow, dec, drv, reach, local, reach0, local0, ent, leave, enter, states, mixed, wb,
-        onehot, pick, len_b, logits, sums, sendbuf, recvbuf, tmbuf, zbuf, ybuf, staged,
+        onehot, pick, len_b, logits, sums, sendbuf, recvbuf, tmbuf, dpbuf,
         x_sem, p1_send, p1_recv, p2_send, p2_recv, xs_send, xs_recv, sib_send, sib_recv,
         reach_send, reach_recv, local_send, local_recv, chain_send, chain_recv, fwd_send,
-        a2a_send, a2a_recv, sum_send, sum_recv, store_sem,
+        a2a_send, a2a_recv, tm_send, tm_recv, dp_send, dp_recv,
     ) = refs
     frames, rows, width = x_ref.shape
     n = math.isqrt(dp_count)
@@ -84,10 +84,11 @@
     def greet(dp_id, tm_id):
         pl.semaphore_signal(barrier, inc=1, device_id=(dp_id, tm_id), device_id_type=MESH)
 
-    for step in range(1, n):
-        greet(dp_of(major, (minor + step) % n), tm)
-    for step in range(1, n):
-        greet(dp_of((major + step) % n, minor), tm)
+    nearest = [o for step in range(1, near + 1) for o in (step, -step)] or [1]
+    for offset in nearest:
+        greet(dp_of(major, (minor + n + offset) % n), tm)
+    for offset in nearest:
+        greet(dp_of((major + n + offset) % n, minor), tm)
     for step in range(1, tm_count):
         greet(me, (tm + step) % tm_count)
 
@@ -113,7 +114,8 @@
         ent[...] = jnp.zeros_like(ent)
 
     recvbuf[...] = jnp.zeros_like(recvbuf)
-    pl.semaphore_wait(barrier, 2 * (n - 1) + (tm_count - 1))
+    dpbuf[...] = jnp.zeros_like(dpbuf)
+    pl.semaphore_wait(barrier, 2 * len(nearest) + (tm_count - 1))
 
     def remote(ref, send, recv, device):
         return pltpu.make_async_remote_copy(
@@ -139,16 +141,34 @@
     def quarters_of(w):
         return pl.ds(firsts[w], counts[w])
 
-    def p1_start(w):
-        for step in range(1, n):
-            remote(
-                wt.at[w, quarters_of(w), y, z], p1_send.at[w], p1_recv.at[w],
-                (dp_of(major, (minor + step) % n), tm),
-            ).start()
-
-    def p1_all(w):
-        some = wt.at[w, quarters_of(w), 0, pl.ds(0, n - 1)]
-        return remote(some, p1_send.at[w], p1_recv.at[w], (me, sibling))
+    def block_of(w, offset):
+        there = (minor + n + offset) % n
+        return wt.at[
+            w, quarters_of(w), major * (1 - core) + there * core,
+            there * (1 - core) + major * core,
+        ]
+
+    def send_block(w, offset, stage, toward):
+        remote(
+            block_of(w, offset), p1_send.at[w], p1_recv.at[w, stage],
+            (dp_of(major, (minor + n + toward) % n), tm),
+        ).start()
+
+    def p1_some(w, stage, count):
+        some = wt.at[w, quarters_of(w), 0, pl.ds(0, count)]
+        return remote(some, p1_send.at[w], p1_recv.at[w, stage], (me, sibling))
+
+    def p1_near(w):
+        for offset in nearest:
+            send_block(w, 0, 0, offset)
+
+    def p1_far(w):
+        p1_some(w, 0, len(nearest)).wait_recv()
+        if n > 2:
+            for step in range(near + 1, n // 2 + 1):
+                send_block(w, near - step, 1, near)
+                if step < n // 2:
+                    send_block(w, step - near, 1, -near)
 
     def p2_all(w):
         some = wt.at[w, quarters_of(w), pl.ds(0, n - 1)]
@@ -160,7 +180,8 @@
         ).start()
 
     def near_sends(w):
-        p1_all(w).wait_recv()
+        if n > 2:
+            p1_some(w, 1, n - 1 - len(nearest)).wait_recv()
 
         def make(c):
             for item in range(1, early + 1):
@@ -250,14 +271,16 @@
             decays(t)
 
     count = len(items)
-    p1_start(0)
+    p1_near(0)
+    p1_far(0)
     narrowing()
     decay_frames(0, 1)
     near_sends(0)
-    p1_start(1)
+    p1_near(1)
     decay_frames(1, 3)
     for item in range(1, early + 1):
         arrive(0, item)
+    p1_far(1)
     near_sends(1)
     decay_frames(3, 4)
     x_done = 0
@@ -440,27 +463,24 @@
 
         outputs(k)
 
-    def share(buffer, own, stage, value, peer_of):
-        buffer[own] = value
-        for step in range(1, buffer.shape[0]):
-            remote(
-                buffer.at[own], sum_send.at[stage], sum_recv.at[stage], peer_of(step)
-            ).start()
-
-    def shared(buffer, stage):
-        return remote(
-            buffer.at[pl.ds(0, buffer.shape[0] - 1)], sum_send.at[stage], sum_recv.at[stage],
-            (me, sibling),
-        )
-
-    def total_of(buffer, stage):
-        shared(buffer, stage).wait_recv()
-        total = buffer[0]
-        for i in range(1, buffer.shape[0]):
-            total = total + buffer[i]
-        return total
-
-    share(tmbuf, tm, 0, sums[...], lambda step: (me, (tm + step) % tm_count))
+    folded = sums[...]
+    folded = folded + pltpu.roll(folded, LANES - 3 * bits, axis=1)
+    folded = (
+        folded + pltpu.roll(folded, LANES - bits, axis=1)
+        + pltpu.roll(folded, LANES - 2 * bits, axis=1)
+    )
+    lane1 = lax.broadcasted_iota(jnp.int32, (1, LANES), 1)
+    is_bit = lane1 < bits
+    one_row = jnp.zeros((1, LANES), jnp.float32)
+    for row in range(4):
+        kept = jnp.where(is_bit, folded[row:row + 1], 0.0)
+        one_row = one_row + (pltpu.roll(kept, row * bits, axis=1) if row else kept)
+    tmbuf[tm, 0:1] = one_row
+    for step in range(1, tm_count):
+        remote(
+            tmbuf.at[tm, pl.ds(0, 1)], tm_send, tm_recv, (me, (tm + step) % tm_count)
+        ).start()
+
     dealt = nn(onehot[...], logits[...])
     sendbuf[...] = dealt.reshape(dp_count, 8, LANES)
     recvbuf[me, 0:GROUP] = sendbuf[me, 0:GROUP]
@@ -468,8 +488,11 @@
     def from_far(i):
         return n // 2 + (i // 2) * (1 - 2 * (i % 2)) - i % 2
 
+    def peer_of(step):
+        return (y + from_far(step // n)) % n * n + (z + from_far(step % n)) % n
+
     def deal(step):
-        peer = (y + from_far(step // n)) % n * n + (z + from_far(step % n)) % n
+        peer = peer_of(step)
         pltpu.make_async_remote_copy(
             src_ref=sendbuf.at[peer, pl.ds(0, GROUP)], dst_ref=recvbuf.at[me, pl.ds(0, GROUP)],
             send_sem=a2a_send, recv_sem=a2a_recv, device_id=(peer, tm), device_id_type=MESH,
@@ -477,17 +500,32 @@
 
     unrolled = 3 if (dp_count - 1) % 3 == 0 else 1
 
-    def deal_some(i, carry):
-        for j in range(unrolled):
-            deal(i * unrolled + j)
-        return carry
-
-    lax.fori_loop(0, (dp_count - 1) // unrolled, deal_some, 0)
-
-    share(zbuf, z, 1, total_of(tmbuf, 0), lambda step: (y * n + (z + step) % n, tm))
+    def for_peers(send):
+        def some(i, carry):
+            for j in range(unrolled):
+                send(i * unrolled + j)
+            return carry
+
+        lax.fori_loop(0, (dp_count - 1) // unrolled, some, 0)
+
+    for_peers(deal)
+    tm_all = remote(tmbuf.at[pl.ds(0, tm_count - 1), pl.ds(0, 1)], tm_send, tm_recv, (me, sibling))
+    tm_all.wait_recv()
+    total = tmbuf[0, 0:1]
+    for i in range(1, tm_count):
+        total = total + tmbuf[i, 0:1]
+    dpbuf[me, 0:1] = total
+
+    def spread(step):
+        remote(
+            dpbuf.at[me, pl.ds(0, 1)], dp_send, dp_recv, (peer_of(step), tm)
+        ).start()
+
+    for_peers(spread)
+    dp_all = remote(dpbuf.at[pl.ds(0, dp_count - 1), pl.ds(0, 1)], dp_send, dp_recv, (me, sibling))
 
     for w in range(2):
-        p1_all(w).wait_send()
+        p1_some(w, 0, n - 1).wait_send()
         p2_all(w).wait_send()
         ours = wt.at[w, pl.ds(2 * core, 2)]
         remote(ours, sib_send.at[w], sib_recv.at[w], (me, sibling)).wait_send()
@@ -515,32 +553,23 @@
     arrived = remote(
         recvbuf.at[pl.ds(0, dp_count - 1), pl.ds(0, GROUP)], a2a_send, a2a_recv, (me, sibling)
     )
-    share(ybuf, y, 2, total_of(zbuf, 1), lambda step: ((y + step) % n * n + z, tm))
-    for stage, buffer in enumerate((tmbuf, zbuf)):
-        shared(buffer, stage).wait_send()
+    tm_all.wait_send()
     arrived.wait_send()
     arrived.wait_recv()
     turned = recvbuf[...].reshape(dp_count * 8, LANES).T.astype(jnp.bfloat16)
     placed = nn(turned, pick[...])
     for t in range(frames):
-        staged[t] = placed[t * bits:(t + 1) * bits, :].astype(jnp.bfloat16)
-    store = pltpu.make_async_copy(staged, codes_ref, store_sem)
-    store.start()
-
-    folded = total_of(ybuf, 2)
-    folded = folded + pltpu.roll(folded, LANES - 3 * bits, axis=1)
-    folded = (
-        folded + pltpu.roll(folded, LANES - bits, axis=1)
-        + pltpu.roll(folded, LANES - 2 * bits, axis=1)
-    )
-    is_bit = lax.broadcasted_iota(jnp.int32, (1, LANES), 1) < bits
-    marginal = jnp.where(is_bit, folded[0:1] / folded[3:4], 0.5)
+        codes_ref[t] = placed[t * bits:(t + 1) * bits, :].astype(jnp.bfloat16)
+
+    dp_all.wait_recv()
+    everything = jnp.sum(dpbuf[...], axis=0)[0:1]
+    parts = [everything] + [pltpu.roll(everything, LANES - row * bits, axis=1) for row in (1, 2, 3)]
+    marginal = jnp.where(is_bit, parts[0] / parts[3], 0.5)
     terms = -marginal * jnp.log(marginal) - (1.0 - marginal) * jnp.log(1.0 - marginal)
     slots = 1.0 / float(rows * dp_count * frames * tm_count)
-    shares = (folded[1:2] + 0.25 * folded[2:3]) * slots - terms
+    shares = (parts[1] + 0.25 * parts[2]) * slots - terms
     penalty_ref[0, 0] = jnp.sum(jnp.where(is_bit, shares, 0.0))
-    shared(ybuf, 2).wait_send()
-    store.wait()
+    dp_all.wait_send()
 
 
 def shards(latents, lengths, plan, w_in, w_down, w_up, w_out, rate, gain, w_bits):
@@ -556,11 +585,11 @@
     codes, penalty = pl.pallas_call(
         functools.partial(kernel, dp_count, tm_count),
         out_shape=(
-            jax.ShapeDtypeStruct((frames, bits, rows), bf16),
+            pltpu.VMEM((frames, bits, rows), bf16),
             jax.ShapeDtypeStruct((1, 1), f32),
         ),
         in_specs=[pl.BlockSpec(memory_space=pl.ANY)] * 10,
-        out_specs=(pl.BlockSpec(memory_space=pl.ANY), pl.BlockSpec(memory_space=pltpu.SMEM)),
+        out_specs=(pl.BlockSpec(memory_space=pltpu.VMEM), pl.BlockSpec(memory_space=pltpu.SMEM)),
         scratch_shapes=[
             pltpu.VMEM((1, rows), jnp.int32),
             pltpu.VMEM((1, rows), jnp.int32),
@@ -595,15 +624,13 @@
             pltpu.VMEM((dp_count, 8, LANES), f32),
             pltpu.VMEM((dp_count, 8, LANES), f32),
             pltpu.VMEM((tm_count, 8, LANES), f32),
-            pltpu.VMEM((n, 8, LANES), f32),
-            pltpu.VMEM((n, 8, LANES), f32),
-            pltpu.VMEM((frames, bits, rows), bf16),
+            pltpu.VMEM((dp_count, 8, LANES), f32),
             dma,
-            dma((2,)), dma((2,)), dma((2,)), dma((2, n)),
+            dma((2,)), dma((2, 2)), dma((2,)), dma((2, n)),
             dma, dma((n + 1,)), dma((2,)), dma((2,)),
             dma, dma, dma((CHUNKS,)), dma((CHUNKS,)),
             dma((PIECES,)), dma((PIECES,)), dma((PIECES,)),
-            dma, dma, dma((3,)), dma((3,)), dma,
+            dma, dma, dma, dma, dma, dma,
         ],
         compiler_params=pltpu.CompilerParams(
             collective_id=0, has_side_effects=True, vmem_limit_bytes=56 * 1024 * 1024

time: 68.7 us -> 73.2 us (1.066)
  Pallas kernels: 64.7 us -> 70.1 us
  local copies, waits for them, and re-layouts: 1.53 us -> 0.65 us
    pallas_call x1, Pallas kernels: 64.7 us -> 70.1 us  [shards(): pl.pallas_call(functools.partial(kernel, dp_count, tm_count), out_shape=(...]
    unnamed x1, local copies, waits for them, and re-layouts: 1.53 us -> 0.65 us
where the time goes in v5:
time: 73.2 us; the launch traced here: 73.1 us
  Pallas kernels  70.1 us (96%)
  between operations  2.33 us (3%)
    pallas_call x1, Pallas kernels, shards(): pl.pallas_call(functools.partial(kernel, dp_count, tm_count), out_shape=(...  70.1 us

profile of v5, /device:TPU:1, one launch (start us, length us, event | category | flops | bytes accessed | tf_op | source)
XLA Modules:
  0.0 73.1 jit_solution(4377924864082629280)
XLA Ops:
  0.6 70.1 %shard_map.113 = (bf16[6,18,256]{2,1,0:T(8,128)(2,1)S(1)}, f32[1,1]{1,0:T(1,128)}) custom-call(bf16[6,256,1024]{2,1,0:T(8,128)(2,1)} %bitcast.12, s32[1,256]{1,0:T(1,128)} %bitcast.19, s32[1,256]{1,0:T(1,128)} %bitcast.20, bf16[16,1024]{1,0:T(8,128)(2,1)} %bitcast.15, bf16[64,1024]{1,0:T(8,128)(2,1)} %bitcast.13, bf16[64,1024]{1,0:T(8,128)(2,1)} %refs_4_.1, ...), custom_call_target="tpu_custom_call" | custom-call | tf_op jit(solution)/shard_map/pallas_call | solution.py:585
  70.7 0.6 copy.12

commit v6 on v4

--- a/solution.py
+++ b/solution.py
@@ -11,7 +11,8 @@
 MESH = pl.DeviceIdType.MESH
 GROUP = 4
 LANES = 128
-CHUNKS = 4
+ENDS = (2, 4, 6, 8)
+CHUNKS = len(ENDS)
 PIECES = 16
 LOG2E = math.log2(math.e)
 
@@ -33,17 +34,18 @@
     small_sem, *refs = refs[9:]
     (
         x_ref, wt, narrow, dec, drv, reach, local, reach0, local0, ent, leave, enter, states, mixed, wb,
-        onehot, pick, len_b, logits, sums, sendbuf, recvbuf, tmbuf, zbuf, ybuf, staged,
+        onehot, pick, len_b, logits, sums, sendbuf, recvbuf, tmbuf, zbuf, ybuf,
         x_sem, p1_send, p1_recv, p2_send, p2_recv, xs_send, xs_recv, sib_send, sib_recv,
         reach_send, reach_recv, local_send, local_recv, chain_send, chain_recv, fwd_send,
-        a2a_send, a2a_recv, sum_send, sum_recv, store_sem,
+        a2a_send, a2a_recv, sum_send, sum_recv,
     ) = refs
     frames, rows, width = x_ref.shape
     n = math.isqrt(dp_count)
     quarter = width // 4
-    part = rows // CHUNKS
     piece = rows // PIECES
-    per_chunk = PIECES // CHUNKS
+    ends = [end * rows // 8 for end in ENDS]
+    starts = [0] + ends[:-1]
+    parts_of = [end - start for start, end in zip(starts, ends)]
     tile = min(256, width)
     tiles = width // tile
     bits = wbits_ref.shape[0]
@@ -285,11 +287,11 @@
         return jnp.concatenate(all_quarters, axis=1)
 
     def valid_of(k, t):
-        rs = slice(k * part, (k + 1) * part)
+        rs = slice(starts[k], ends[k])
         return jnp.where(len_b[rs, :] > float(t), 1.0, 0.0)
 
     def drives(k):
-        rs = slice(k * part, (k + 1) * part)
+        rs, part = slice(starts[k], ends[k]), parts_of[k]
         left_side = x_ref[:, rs, :].reshape(frames * part, width)
         for i in range(tiles):
             cols = slice(i * tile, (i + 1) * tile)
@@ -305,15 +307,14 @@
         @pl.when(core == 0)
         def _():
             pltpu.make_async_remote_copy(
-                src_ref=local.at[pl.ds(k * part, part)], dst_ref=local0.at[pl.ds(k * part, part)],
+                src_ref=local.at[pl.ds(starts[k], part)], dst_ref=local0.at[pl.ds(starts[k], part)],
                 send_sem=local_send.at[k], recv_sem=local_recv.at[k],
                 device_id=(me, sibling), device_id_type=MESH,
             ).start()
 
     def local_wait(k):
-        remote(
-            local0.at[pl.ds(k * part, part)], local_send.at[k], local_recv.at[k], (me, sibling)
-        ).wait_recv()
+        rs = pl.ds(starts[k], parts_of[k])
+        remote(local0.at[rs], local_send.at[k], local_recv.at[k], (me, sibling)).wait_recv()
 
     def reach_wait():
         remote(reach0, reach_send, reach_recv, (me, sibling)).wait_recv()
@@ -339,14 +340,15 @@
         if k == 0:
             reach_wait()
         local_wait(k)
-        for j in range(k * per_chunk, (k + 1) * per_chunk):
+        for j in range(starts[k] // piece, ends[k] // piece):
             pass_on(j, sends, receives)
 
     def pass_half(h):
         if h == 0:
             reach_wait()
-        for k in range(h * CHUNKS // 2, (h + 1) * CHUNKS // 2):
-            local_wait(k)
+        for k in range(CHUNKS):
+            if (starts[k] >= rows // 2) == (h == 1):
+                local_wait(k)
 
         def step(j, carry):
             pass_on(j)
@@ -355,23 +357,24 @@
         lax.fori_loop(h * PIECES // 2, (h + 1) * PIECES // 2, step, 0)
 
     def outputs(k):
-        rs = slice(k * part, (k + 1) * part)
+        rs, part = slice(starts[k], ends[k]), parts_of[k]
+        count = frames * part
         for i in range(tiles):
             cols = slice(i * tile, (i + 1) * tile)
             s = enter[rs, cols]
             for t in range(frames):
                 s = dec[t, rs, cols] * s + drv[t, rs, cols]
-                states[t, :, cols] = s.astype(jnp.bfloat16)
-        left_side = states[...].reshape(frames * part, width)
+                states[t, 0:part, cols] = s.astype(jnp.bfloat16)
+        left_side = states[:, 0:part].reshape(count, width)
         square = None
         for i in range(tiles):
             cols = slice(i * tile, (i + 1) * tile)
-            x = x_ref[:, rs, cols].reshape(frames * part, tile).astype(jnp.float32)
+            x = x_ref[:, rs, cols].reshape(count, tile).astype(jnp.float32)
             m = x + nt(left_side, weight_rows(1, i))
-            mixed[:, cols] = m
+            mixed[0:count, cols] = m
             square = m * m if i == 0 else square + m * m
         scaling = lax.rsqrt(jnp.sum(square, axis=1, keepdims=True) * (1.0 / width) + 1e-06)
-        normed = (mixed[...] * scaling * gain_ref[...]).astype(jnp.bfloat16)
+        normed = (mixed[0:count] * scaling * gain_ref[...]).astype(jnp.bfloat16)
         by_frame = nt(normed, wb[...])
         values = by_frame[0:part]
         for t in range(1, frames):
@@ -431,7 +434,7 @@
 
         @pl.when(core == 0)
         def _():
-            for j in range(k * per_chunk, (k + 1) * per_chunk):
+            for j in range(starts[k] // piece, ends[k] // piece):
                 @pl.when(chip > 0)
                 def _():
                     remote(ent.at[j], fwd_send.at[j], chain_recv.at[j], (me, sibling)).wait_recv()
@@ -440,27 +443,39 @@
 
         outputs(k)
 
+    folded = sums[...]
+    folded = folded + pltpu.roll(folded, LANES - 3 * bits, axis=1)
+    folded = (
+        folded + pltpu.roll(folded, LANES - bits, axis=1)
+        + pltpu.roll(folded, LANES - 2 * bits, axis=1)
+    )
+    is_bit = lax.broadcasted_iota(jnp.int32, (1, LANES), 1) < bits
+    one_row = jnp.zeros((1, LANES), jnp.float32)
+    for row in range(4):
+        kept = jnp.where(is_bit, folded[row:row + 1], 0.0)
+        one_row = one_row + (pltpu.roll(kept, row * bits, axis=1) if row else kept)
+
     def share(buffer, own, stage, value, peer_of):
-        buffer[own] = value
+        buffer[own, 0:1] = value
         for step in range(1, buffer.shape[0]):
             remote(
-                buffer.at[own], sum_send.at[stage], sum_recv.at[stage], peer_of(step)
+                buffer.at[own, pl.ds(0, 1)], sum_send.at[stage], sum_recv.at[stage], peer_of(step)
             ).start()
 
     def shared(buffer, stage):
         return remote(
-            buffer.at[pl.ds(0, buffer.shape[0] - 1)], sum_send.at[stage], sum_recv.at[stage],
+            buffer.at[pl.ds(0, buffer.shape[0] - 1), pl.ds(0, 1)], sum_send.at[stage], sum_recv.at[stage],
             (me, sibling),
         )
 
     def total_of(buffer, stage):
         shared(buffer, stage).wait_recv()
-        total = buffer[0]
+        total = buffer[0, 0:1]
         for i in range(1, buffer.shape[0]):
-            total = total + buffer[i]
+            total = total + buffer[i, 0:1]
         return total
 
-    share(tmbuf, tm, 0, sums[...], lambda step: (me, (tm + step) % tm_count))
+    share(tmbuf, tm, 0, one_row, lambda step: (me, (tm + step) % tm_count))
     dealt = nn(onehot[...], logits[...])
     sendbuf[...] = dealt.reshape(dp_count, 8, LANES)
     recvbuf[me, 0:GROUP] = sendbuf[me, 0:GROUP]
@@ -497,9 +512,8 @@
     def _():
         remote(reach, reach_send, reach_recv, (me, sibling)).wait_send()
         for k in range(CHUNKS):
-            remote(
-                local.at[pl.ds(k * part, part)], local_send.at[k], local_recv.at[k], (me, sibling)
-            ).wait_send()
+            rs = pl.ds(starts[k], parts_of[k])
+            remote(local.at[rs], local_send.at[k], local_recv.at[k], (me, sibling)).wait_send()
 
     @pl.when(is_core1)
     def _():
@@ -523,24 +537,16 @@
     turned = recvbuf[...].reshape(dp_count * 8, LANES).T.astype(jnp.bfloat16)
     placed = nn(turned, pick[...])
     for t in range(frames):
-        staged[t] = placed[t * bits:(t + 1) * bits, :].astype(jnp.bfloat16)
-    store = pltpu.make_async_copy(staged, codes_ref, store_sem)
-    store.start()
-
-    folded = total_of(ybuf, 2)
-    folded = folded + pltpu.roll(folded, LANES - 3 * bits, axis=1)
-    folded = (
-        folded + pltpu.roll(folded, LANES - bits, axis=1)
-        + pltpu.roll(folded, LANES - 2 * bits, axis=1)
-    )
-    is_bit = lax.broadcasted_iota(jnp.int32, (1, LANES), 1) < bits
-    marginal = jnp.where(is_bit, folded[0:1] / folded[3:4], 0.5)
+        codes_ref[t] = placed[t * bits:(t + 1) * bits, :].astype(jnp.bfloat16)
+
+    everything = total_of(ybuf, 2)
+    parts = [everything] + [pltpu.roll(everything, LANES - row * bits, axis=1) for row in (1, 2, 3)]
+    marginal = jnp.where(is_bit, parts[0] / parts[3], 0.5)
     terms = -marginal * jnp.log(marginal) - (1.0 - marginal) * jnp.log(1.0 - marginal)
     slots = 1.0 / float(rows * dp_count * frames * tm_count)
-    shares = (folded[1:2] + 0.25 * folded[2:3]) * slots - terms
+    shares = (parts[1] + 0.25 * parts[2]) * slots - terms
     penalty_ref[0, 0] = jnp.sum(jnp.where(is_bit, shares, 0.0))
     shared(ybuf, 2).wait_send()
-    store.wait()
 
 
 def shards(latents, lengths, plan, w_in, w_down, w_up, w_out, rate, gain, w_bits):
@@ -549,18 +555,18 @@
     n = math.isqrt(dp_count)
     bits = w_bits.shape[1]
     narrow_width = w_down.shape[1]
-    part = rows // CHUNKS
+    part = rows // 4
     block = width // dp_count
     bf16, f32 = jnp.bfloat16, jnp.float32
     dma = pltpu.SemaphoreType.DMA
     codes, penalty = pl.pallas_call(
         functools.partial(kernel, dp_count, tm_count),
         out_shape=(
-            jax.ShapeDtypeStruct((frames, bits, rows), bf16),
+            pltpu.VMEM((frames, bits, rows), bf16),
             jax.ShapeDtypeStruct((1, 1), f32),
         ),
         in_specs=[pl.BlockSpec(memory_space=pl.ANY)] * 10,
-        out_specs=(pl.BlockSpec(memory_space=pl.ANY), pl.BlockSpec(memory_space=pltpu.SMEM)),
+        out_specs=(pl.BlockSpec(memory_space=pltpu.VMEM), pl.BlockSpec(memory_space=pltpu.SMEM)),
         scratch_shapes=[
             pltpu.VMEM((1, rows), jnp.int32),
             pltpu.VMEM((1, rows), jnp.int32),
@@ -597,13 +603,12 @@
             pltpu.VMEM((tm_count, 8, LANES), f32),
             pltpu.VMEM((n, 8, LANES), f32),
             pltpu.VMEM((n, 8, LANES), f32),
-            pltpu.VMEM((frames, bits, rows), bf16),
             dma,
             dma((2,)), dma((2,)), dma((2,)), dma((2, n)),
             dma, dma((n + 1,)), dma((2,)), dma((2,)),
             dma, dma, dma((CHUNKS,)), dma((CHUNKS,)),
             dma((PIECES,)), dma((PIECES,)), dma((PIECES,)),
-            dma, dma, dma((3,)), dma((3,)), dma,
+            dma, dma, dma((3,)), dma((3,)),
         ],
         compiler_params=pltpu.CompilerParams(
             collective_id=0, has_side_effects=True, vmem_limit_bytes=56 * 1024 * 1024

time: 68.7 us -> 67.4 us (0.981)
  local copies, waits for them, and re-layouts: 1.53 us -> 0.65 us
  Pallas kernels: 64.7 us -> 64 us
    unnamed x1, local copies, waits for them, and re-layouts: 1.53 us -> 0.65 us
where the time goes in v6:
time: 67.4 us; the launch traced here: 67 us
  Pallas kernels  64 us (95%)
  between operations  2.33 us (3%)
    pallas_call x1, Pallas kernels, shards(): pl.pallas_call(functools.partial(kernel, dp_count, tm_count), out_shape=(...  64 us

profile of v6, /device:TPU:1, one launch (start us, length us, event | category | flops | bytes accessed | tf_op | source)
XLA Modules:
  0.0 67.0 jit_solution(6839879309179847867)
XLA Ops:
  0.6 64.0 %shard_map.113 = (bf16[6,18,256]{2,1,0:T(8,128)(2,1)S(1)}, f32[1,1]{1,0:T(1,128)}) custom-call(bf16[6,256,1024]{2,1,0:T(8,128)(2,1)} %bitcast.12, s32[1,256]{1,0:T(1,128)} %bitcast.19, s32[1,256]{1,0:T(1,128)} %bitcast.20, bf16[16,1024]{1,0:T(8,128)(2,1)} %bitcast.15, bf16[64,1024]{1,0:T(8,128)(2,1)} %bitcast.13, bf16[64,1024]{1,0:T(8,128)(2,1)} %refs_4_.1, ...), custom_call_target="tpu_custom_call" | custom-call | tf_op jit(solution)/shard_map/pallas_call | solution.py:562
  64.7 0.6 copy.12

commit v7 on v6

--- a/solution.py
+++ b/solution.py
@@ -11,7 +11,7 @@
 MESH = pl.DeviceIdType.MESH
 GROUP = 4
 LANES = 128
-ENDS = (2, 4, 6, 8)
+ENDS = (2, 5, 8)
 CHUNKS = len(ENDS)
 PIECES = 16
 LOG2E = math.log2(math.e)
@@ -555,7 +555,7 @@
     n = math.isqrt(dp_count)
     bits = w_bits.shape[1]
     narrow_width = w_down.shape[1]
-    part = rows // 4
+    part = rows * 3 // 8
     block = width // dp_count
     bf16, f32 = jnp.bfloat16, jnp.float32
     dma = pltpu.SemaphoreType.DMA

time: 67.4 us -> 67.4 us (level)
  no operation moved by 1% of the time
where the time goes in v7:
time: 67.4 us; the launch traced here: 67.1 us
  Pallas kernels  64.1 us (95%)
  between operations  2.33 us (3%)
    pallas_call x1, Pallas kernels, shards(): pl.pallas_call(functools.partial(kernel, dp_count, tm_count), out_shape=(...  64.1 us

profile of v7, /device:TPU:1, one launch (start us, length us, event | category | flops | bytes accessed | tf_op | source)
XLA Modules:
  0.0 67.1 jit_solution(10716586191322046084)
XLA Ops:
  0.6 64.1 %shard_map.113 = (bf16[6,18,256]{2,1,0:T(8,128)(2,1)S(1)}, f32[1,1]{1,0:T(1,128)}) custom-call(bf16[6,256,1024]{2,1,0:T(8,128)(2,1)} %bitcast.12, s32[1,256]{1,0:T(1,128)} %bitcast.19, s32[1,256]{1,0:T(1,128)} %bitcast.20, bf16[16,1024]{1,0:T(8,128)(2,1)} %bitcast.15, bf16[64,1024]{1,0:T(8,128)(2,1)} %bitcast.13, bf16[64,1024]{1,0:T(8,128)(2,1)} %refs_4_.1, ...), custom_call_target="tpu_custom_call" | custom-call | tf_op jit(solution)/shard_map/pallas_call | solution.py:562
  64.7 0.6 copy.12
